TPU v7x, 32 devices: a whole 2x2x4 slice. The times are simulated.
32 devices in a mesh: wide: 2 (over y), blk: 4 (over z), head: 4 (over x, core).
Axes of the slice: x: 2, y: 2, z: 4, core: 2. Of those that a mesh axis runs over, the one named last changes fastest.
Arguments:
- tokens: bfloat16 [8, 4, 256, 1536], P('blk', 'wide', 'head'), may hold values from -6 to 6
- positions: int32 [8, 4, 256], P('blk', 'wide', 'head'), may hold values from 0 to 2047, as said below
- block_order: int32 [8], replicated, may hold values from 0 to 7, as said below
- w_qkv: bfloat16 [1536, 2048], P('wide'), may hold values from -0.15625 to 0.15625
- qkv_bias: bfloat16 [2048], P('wide'), may hold values from -0.59765625 to 0.59765625
- w_out: bfloat16 [1536, 1536], P('wide'), may hold values from -0.875 to 0.875
- w_gate_up: bfloat16 [1536, 17920], P('wide'), may hold values from -0.15625 to 0.15625
- w_down: bfloat16 [1536, 8960], P('wide'), may hold values from -0.0625 to 0.0625
- gain_attn: bfloat16 [1536], P('wide'), may hold values from 0.25 to 1.75
- gain_mlp: bfloat16 [1536], P('wide'), may hold values from 0.25 to 1.75
- cotangent: bfloat16 [8, 4, 256, 1536], P('blk', 'wide', 'head'), may hold values from -6 to 6
Outputs:
- output: bfloat16 [8, 4, 256, 1536], P('blk', 'wide', 'head')
- input_grad: bfloat16 [8, 4, 256, 1536], P('blk', 'wide', 'head')
- qkv_grad: float32 [1536, 2048], P('wide')
- bias_grad: float32 [2048], P('wide')
- out_grad: float32 [1536, 1536], P('wide')
- gate_up_grad: float32 [1536, 17920], P('wide')
- down_grad: float32 [1536, 8960], P('wide')
- gain_attn_grad: float32 [1536], P('wide')
- gain_mlp_grad: float32 [1536], P('wide')
Inputs may be any that keep to these rules, and one draw needn't show every extreme that they name: Each number from 0 to 7 stands once; slot j of every sequence holds that sequence's block number block_order[j], 256 consecutive tokens. Read in the order of block numbers, a sequence's positions count 0, 1, 2, ... from its first token and restart at 0 at the first token of each packed document; one sequence is a single document that counts to 2047.
All inputs are finite; a program needn't handle non-finite values.
Results may differ from a plain program's by a relative error of at most 0.017.
Values may be sent and summed in bfloat16 or wider, within the bound.
No kernel may reach another device: no remote copies, remote signals or barrier semaphores. Data moves between devices by JAX's collectives and lax.ppermute only.
A program may use at most 704 MiB of HBM per device.

v0:
```python
import jax
import jax.numpy as jnp
from jax import lax
from jax.sharding import PartitionSpec as P

QUERY_HEADS = 12
KEY_VALUE_HEADS = 2
HEAD_SIZE = 128


norm_eps = 1e-06
rope_theta = 1000000.0
masked_score = -1e30


def rms_parts(values, gain_row):
    inverse = lax.rsqrt(jnp.mean(values * values, axis=-1, keepdims=True) + norm_eps)
    scaled = values * inverse
    return (scaled * gain_row, scaled, inverse)


def rms_back(grad_normed, scaled, inverse, gain_row):
    grad_scaled = grad_normed * gain_row
    mean_term = jnp.mean(grad_scaled * scaled, axis=-1, keepdims=True)
    return (inverse * (grad_scaled - scaled * mean_term), jnp.sum(grad_normed * scaled, axis=0))


def half_turn(values):
    half_size = values.shape[-1] // 2
    return jnp.concatenate([-values[..., half_size:], values[..., :half_size]], axis=-1)


def rotate_pairs(values, cosine_table, sine_values):
    return values * cosine_table + half_turn(values) * sine_values


def turn_back(values, cosine_table, sine_values):
    return values * cosine_table - half_turn(values * sine_values)


def rope_tables(positions):
    frequency = rope_theta ** (-jnp.arange(0, HEAD_SIZE, 2).astype(jnp.float32) / HEAD_SIZE)
    angles = positions.astype(jnp.float32)[:, None] * frequency[None, :]
    angles = jnp.concatenate([angles, angles], axis=-1)
    return (jnp.cos(angles), jnp.sin(angles))


def slot_orders(block_order, wanted):
    table_index = jnp.arange(block_order.shape[0], dtype=jnp.int32)
    return jnp.sum(
        jnp.where(table_index[None, :] == wanted[:, None], block_order[None, :], 0), axis=1
    )


def visible_mask(query_order, key_order, row_count):
    row_index = jnp.arange(row_count, dtype=jnp.int32)
    earlier = (key_order < query_order)[:, None, None]
    same_block = (key_order == query_order)[:, None, None]
    causal = (row_index[None, :] <= row_index[:, None])[None]
    return (earlier | same_block & causal)[:, None, :, None, :]


def on_device(
    tokens,
    positions,
    block_order,
    w_qkv,
    qkv_bias,
    w_out,
    w_gate_up,
    w_down,
    gain_attn,
    gain_mlp,
    cotangent,
):
    slot_count, seq_count, rows_dev, model_width = tokens.shape
    head_shard_count = lax.axis_size("head")
    query_total_width = QUERY_HEADS * HEAD_SIZE
    key_value_width = KEY_VALUE_HEADS * HEAD_SIZE
    heads_here = QUERY_HEADS // head_shard_count
    key_value_share = head_shard_count // KEY_VALUE_HEADS
    q_here = heads_here * HEAD_SIZE
    block_row_set = rows_dev * head_shard_count
    full_qkv, full_out, full_gate_up, full_down, full_bias, full_gain_attn, full_gain_mlp = (
        lax.all_gather(w_qkv, "wide", axis=0, tiled=True),
        lax.all_gather(w_out, "wide", axis=0, tiled=True),
        lax.all_gather(w_gate_up, "wide", axis=0, tiled=True),
        lax.all_gather(w_down, "wide", axis=0, tiled=True),
        lax.all_gather(qkv_bias, "wide", axis=0, tiled=True),
        lax.all_gather(gain_attn, "wide", axis=0, tiled=True),
        lax.all_gather(gain_mlp, "wide", axis=0, tiled=True),
    )
    gain_attn_row = full_gain_attn.astype(jnp.float32)
    gain_mlp_row = full_gain_mlp.astype(jnp.float32)
    bias_row = full_bias.astype(jnp.float32)
    flat_tokens = tokens.reshape(-1, model_width).astype(jnp.float32)
    normed_attn, scaled_attn, inverse_attn = rms_parts(flat_tokens, gain_attn_row)
    normed_attn = normed_attn.astype(jnp.bfloat16)
    projected_rows = jnp.dot(normed_attn, full_qkv, preferred_element_type=jnp.float32) + bias_row
    cosine_table, sine_values = rope_tables(positions.reshape(-1))
    queries = rotate_pairs(
        projected_rows[:, :query_total_width].reshape(-1, QUERY_HEADS, HEAD_SIZE),
        cosine_table[:, None, :],
        sine_values[:, None, :],
    )
    key_row_set = rotate_pairs(
        projected_rows[:, query_total_width : query_total_width + key_value_width].reshape(
            -1, KEY_VALUE_HEADS, HEAD_SIZE
        ),
        cosine_table[:, None, :],
        sine_values[:, None, :],
    )
    value_row_set = projected_rows[:, query_total_width + key_value_width :].reshape(
        -1, KEY_VALUE_HEADS, HEAD_SIZE
    )
    pair_rows = jnp.repeat(
        jnp.concatenate([key_row_set, value_row_set], axis=-1), key_value_share, axis=1
    )
    query_send = queries.astype(jnp.bfloat16).reshape(
        slot_count, seq_count, rows_dev, head_shard_count, q_here
    )
    pair_send = pair_rows.astype(jnp.bfloat16).reshape(
        slot_count, seq_count, rows_dev, head_shard_count, 2 * HEAD_SIZE
    )
    query_heads, pair_heads = (
        lax.all_to_all(query_send, "head", split_axis=3, concat_axis=2, tiled=True),
        lax.all_to_all(pair_send, "head", split_axis=3, concat_axis=2, tiled=True),
    )
    query_heads = query_heads.reshape(slot_count, seq_count, block_row_set, heads_here, HEAD_SIZE)
    own_slots = lax.axis_index("blk") * slot_count + jnp.arange(slot_count, dtype=jnp.int32)
    query_order = slot_orders(block_order, own_slots)
    score_scale = HEAD_SIZE ** (-0.5)
    every_pair = lax.all_gather(pair_heads, "blk", axis=0, tiled=True)
    stat_shape = (slot_count, seq_count, block_row_set, heads_here)
    state_now = (
        jnp.full(stat_shape, masked_score, jnp.float32),
        jnp.zeros(stat_shape, jnp.float32),
        jnp.zeros(stat_shape + (HEAD_SIZE,), jnp.float32),
    )
    for slot_number in range(every_pair.shape[0]):
        kv_slot = every_pair[slot_number]
        attend_run_peak, attend_run_total, attend_run_accum = state_now
        attend_key_block = kv_slot[:, :, 0, :HEAD_SIZE]
        attend_value_block = kv_slot[:, :, 0, HEAD_SIZE:]
        attend_scores = (
            jnp.einsum(
                "asrhd,skd->asrhk",
                query_heads,
                attend_key_block,
                preferred_element_type=jnp.float32,
            )
            * score_scale
        )
        attend_allowed = visible_mask(query_order, block_order[slot_number], block_row_set)
        masked = jnp.where(attend_allowed, attend_scores, masked_score)
        new_peak = jnp.maximum(attend_run_peak, jnp.max(masked, axis=-1))
        weights = jnp.where(attend_allowed, jnp.exp(masked - new_peak[..., None]), 0.0)
        rescale = jnp.exp(attend_run_peak - new_peak)
        attend_run_total = attend_run_total * rescale + jnp.sum(weights, axis=-1)
        attend_run_accum = attend_run_accum * rescale[..., None] + jnp.einsum(
            "asrhk,skd->asrhd",
            weights.astype(jnp.bfloat16),
            attend_value_block,
            preferred_element_type=jnp.float32,
        )
        state_now = (new_peak, attend_run_total, attend_run_accum)
    run_peak, run_total, run_accum = state_now
    attention = run_accum / run_total[..., None]
    log_total = run_peak + jnp.log(run_total)
    attention_send = attention.astype(jnp.bfloat16).reshape(
        slot_count, seq_count, block_row_set, 1, q_here
    )
    attended = lax.all_to_all(
        attention_send, "head", split_axis=2, concat_axis=3, tiled=True
    ).reshape(-1, query_total_width)
    branch = jnp.einsum("nc,dc->nd", attended, full_out, preferred_element_type=jnp.float32)
    middle = flat_tokens + branch
    normed_mlp, scaled_mlp, inverse_mlp = rms_parts(middle, gain_mlp_row)
    normed_mlp = normed_mlp.astype(jnp.bfloat16)
    cot_in = cotangent.reshape(-1, model_width)
    ff_width = full_down.shape[1]
    gate_up = jnp.dot(normed_mlp, full_gate_up, preferred_element_type=jnp.float32)
    gate_part = gate_up[:, :ff_width]
    up_part = gate_up[:, ff_width:]
    gate_sigmoid = jax.nn.sigmoid(gate_part)
    gate_silu = gate_part * gate_sigmoid
    hidden = (gate_silu * up_part).astype(jnp.bfloat16)
    mlp_part = jnp.einsum("nf,df->nd", hidden, full_down, preferred_element_type=jnp.float32)
    grad_hidden = jnp.dot(cot_in, full_down, preferred_element_type=jnp.float32)
    grad_gate = grad_hidden * up_part * gate_sigmoid * (1.0 + gate_part * (1.0 - gate_sigmoid))
    grad_up = grad_hidden * gate_silu
    grad_gate_up = jnp.concatenate([grad_gate, grad_up], axis=1).astype(jnp.bfloat16)
    grad_mlp_part = jnp.einsum(
        "nf,df->nd", grad_gate_up, full_gate_up, preferred_element_type=jnp.float32
    )
    output = (middle + mlp_part).astype(jnp.bfloat16).reshape(tokens.shape)
    grad_output = cotangent.reshape(-1, model_width).astype(jnp.float32)
    grad_middle_part, grad_gain_mlp = rms_back(grad_mlp_part, scaled_mlp, inverse_mlp, gain_mlp_row)
    grad_middle = grad_output + grad_middle_part
    grad_branch = grad_middle.astype(jnp.bfloat16)
    grad_attended = jnp.dot(grad_branch, full_out, preferred_element_type=jnp.float32).astype(
        jnp.bfloat16
    )
    grad_send = grad_attended.reshape(slot_count, seq_count, rows_dev, head_shard_count, q_here)
    grad_heads = lax.all_to_all(grad_send, "head", split_axis=3, concat_axis=2, tiled=True).reshape(
        slot_count, seq_count, block_row_set, heads_here, HEAD_SIZE
    )
    row_inner = jnp.sum(grad_heads.astype(jnp.float32) * attention, axis=-1)
    grad_queries = jnp.zeros(stat_shape + (HEAD_SIZE,), jnp.float32)
    key_terms = []
    for slot_number in range(every_pair.shape[0]):
        key_block = every_pair[slot_number, :, :, 0, :HEAD_SIZE]
        value_block = every_pair[slot_number, :, :, 0, HEAD_SIZE:]
        scores = (
            jnp.einsum(
                "asrhd,skd->asrhk", query_heads, key_block, preferred_element_type=jnp.float32
            )
            * score_scale
        )
        allowed = visible_mask(query_order, block_order[slot_number], block_row_set)
        probs = jnp.where(
            allowed, jnp.exp(jnp.where(allowed, scores, masked_score) - log_total[..., None]), 0.0
        )
        grad_probs = jnp.einsum(
            "asrhd,skd->asrhk", grad_heads, value_block, preferred_element_type=jnp.float32
        )
        grad_scores = (probs * (grad_probs - row_inner[..., None])).astype(jnp.bfloat16)
        grad_queries = (
            grad_queries
            + jnp.einsum(
                "asrhk,skd->asrhd", grad_scores, key_block, preferred_element_type=jnp.float32
            )
            * score_scale
        )
        grad_keys = (
            jnp.einsum(
                "asrhk,asrhd->skd", grad_scores, query_heads, preferred_element_type=jnp.float32
            )
            * score_scale
        )
        grad_values = jnp.einsum(
            "asrhk,asrhd->skd",
            probs.astype(jnp.bfloat16),
            grad_heads,
            preferred_element_type=jnp.float32,
        )
        key_terms.append(jnp.concatenate([grad_keys, grad_values], axis=-1))
    key_terms = jnp.stack(key_terms)[:, :, :, None, :]
    key_grads = lax.psum_scatter(
        key_terms.astype(jnp.bfloat16), "blk", scatter_dimension=0, tiled=True
    ).astype(jnp.float32)
    query_back = grad_queries.reshape(slot_count, seq_count, block_row_set, 1, q_here)
    back_queries, backward_pairs = (
        lax.all_to_all(
            query_back.astype(jnp.bfloat16), "head", split_axis=2, concat_axis=3, tiled=True
        ).astype(query_back.dtype),
        lax.all_to_all(
            key_grads.astype(jnp.bfloat16), "head", split_axis=2, concat_axis=3, tiled=True
        ).astype(key_grads.dtype),
    )
    back_queries = back_queries.reshape(-1, QUERY_HEADS, HEAD_SIZE)
    backward_pairs = jnp.sum(
        backward_pairs.reshape(-1, KEY_VALUE_HEADS, key_value_share, 2 * HEAD_SIZE), axis=2
    )
    grad_projected = jnp.concatenate(
        [
            turn_back(back_queries, cosine_table[:, None, :], sine_values[:, None, :]).reshape(
                -1, query_total_width
            ),
            turn_back(
                backward_pairs[..., :HEAD_SIZE], cosine_table[:, None, :], sine_values[:, None, :]
            ).reshape(-1, key_value_width),
            backward_pairs[..., HEAD_SIZE:].reshape(-1, key_value_width),
        ],
        axis=1,
    ).astype(jnp.bfloat16)
    grad_bias = jnp.sum(grad_projected.astype(jnp.float32), axis=0)
    grad_normed_attn = jnp.einsum(
        "nc,dc->nd", grad_projected, full_qkv, preferred_element_type=jnp.float32
    )
    grad_flat, grad_gain_attn = rms_back(grad_normed_attn, scaled_attn, inverse_attn, gain_attn_row)
    input_grad = (grad_middle + grad_flat).astype(jnp.bfloat16).reshape(tokens.shape)
    part_rows = lax.psum_scatter(
        jnp.concatenate(
            [
                jnp.einsum(
                    "nc,nk->ck", normed_attn, grad_projected, preferred_element_type=jnp.float32
                ),
                jnp.einsum("nc,nk->ck", grad_branch, attended, preferred_element_type=jnp.float32),
                jnp.einsum(
                    "nc,nk->ck", normed_mlp, grad_gate_up, preferred_element_type=jnp.float32
                ),
                jnp.einsum("nc,nk->ck", cot_in, hidden, preferred_element_type=jnp.float32),
            ],
            axis=1,
        ),
        ("wide", "blk", "head"),
        scatter_dimension=0,
        tiled=True,
    )
    bias_part, attn_gain_part, mlp_gain_part = (
        lax.psum_scatter(grad_bias, ("wide", "blk", "head"), scatter_dimension=0, tiled=True),
        lax.psum_scatter(grad_gain_attn, ("wide", "blk", "head"), scatter_dimension=0, tiled=True),
        lax.psum_scatter(grad_gain_mlp, ("wide", "blk", "head"), scatter_dimension=0, tiled=True),
    )
    stacked, bias_grad, gain_attn_grad, gain_mlp_grad = (
        lax.all_gather(
            part_rows[None].astype(jnp.bfloat16), ("blk", "head"), axis=0, tiled=True
        ).astype(jnp.float32),
        lax.all_gather(bias_part.astype(jnp.bfloat16), ("blk", "head"), axis=0, tiled=True).astype(
            bias_part.dtype
        ),
        lax.all_gather(
            attn_gain_part.astype(jnp.bfloat16), ("blk", "head"), axis=0, tiled=True
        ).astype(attn_gain_part.dtype),
        lax.all_gather(
            mlp_gain_part.astype(jnp.bfloat16), ("blk", "head"), axis=0, tiled=True
        ).astype(mlp_gain_part.dtype),
    )
    shard_rows = stacked.reshape(-1, stacked.shape[2])
    qkv_width = full_qkv.shape[1]
    out_width = full_out.shape[1]
    gate_up_width = full_gate_up.shape[1]
    qkv_grad = shard_rows[:, :qkv_width]
    out_grad = shard_rows[:, qkv_width : qkv_width + out_width]
    gate_up_grad = shard_rows[:, qkv_width + out_width : qkv_width + out_width + gate_up_width]
    down_grad = shard_rows[:, qkv_width + out_width + gate_up_width :]
    return (
        output,
        input_grad,
        qkv_grad,
        bias_grad,
        out_grad,
        gate_up_grad,
        down_grad,
        gain_attn_grad,
        gain_mlp_grad,
    )


def solution(mesh):
    in_specs = (
        P("blk", "wide", "head", None),
        P("blk", "wide", "head"),
        P(),
        P("wide", None),
        P("wide"),
        P("wide", None),
        P("wide", None),
        P("wide", None),
        P("wide"),
        P("wide"),
        P("blk", "wide", "head", None),
    )
    out_specs = (
        P("blk", "wide", "head", None),
        P("blk", "wide", "head", None),
        P("wide", None),
        P("wide"),
        P("wide", None),
        P("wide", None),
        P("wide", None),
        P("wide"),
        P("wide"),
    )
    return jax.shard_map(
        on_device, mesh=mesh, in_specs=in_specs, out_specs=out_specs, check_vma=False
    )
```

profile of v0, /device:TPU:0, one launch (start us, length us, event | category | flops | bytes accessed | tf_op | source)
XLA Modules:
  0.0 3364.0 jit_solution(16893993605870762909)
XLA Ops:
  19.3 73.4 %all-gather.10.cloned.1.call-done = bf16[1536,2048]{1,0:T(8,128)(2,1)} async-done(((bf16[768,2048]{1,0:T(8,128)(2,1)}), bf16[1536,2048]{1,0:T(8,128)(2,1)}) %all-gather.10.cloned.1.call-update) | async-done | bytes 6291472 | tf_op jit(solution)/shard_map/all_gather | solution.py:85
  97.8 11.4 all_to_all.81
  149.4 5.8 all-gather.12.cloned.1.call-done
  200.8 12.8 fusion.75
  222.0 630.1 %all-gather.16.cloned.1.call-done = bf16[1536,17920]{1,0:T(8,128)(2,1)} async-done(((bf16[768,17920]{1,0:T(8,128)(2,1)}), bf16[1536,17920]{1,0:T(8,128)(2,1)}) %all-gather.16.cloned.1.call-update) | async-done | bytes 55050256 | tf_op jit(solution)/shard_map/all_gather | solution.py:87
  852.1 37.1 %fusion.362 = f32[256,17920]{1,0:T(8,128)} fusion(bf16[1536,17920]{1,0:T(8,128)(2,1)} %all-gather.16.cloned.1.call-done, f32[256,1536]{1,0:T(8,128)S(1)} %get-tuple-element.117, f32[1536]{0:T(1024)S(1)} %reshape.720, f32[256]{0:T(256)S(1)} %add_rsqrt_fusion.1), kind=kOutput, calls=%fused_computation.456 | convolution fusion | flops 14094041088 | bytes 74980352 | tf_op jit(solution)/shard_map/dot_general | solution.py:182
  889.3 286.4 %all-gather.18.cloned.1.call-done = bf16[1536,8960]{1,0:T(8,128)(2,1)} async-done(((bf16[768,8960]{1,0:T(8,128)(2,1)}), bf16[1536,8960]{1,0:T(8,128)(2,1)}) %all-gather.18.cloned.1.call-update) | async-done | bytes 27525136 | tf_op jit(solution)/shard_map/all_gather | solution.py:88
  1175.7 25.2 multiply_convert_fusion.1
  1200.8 25.6 multiply_reduce_fusion
  1242.5 40.4 %fusion.1 = f32[1536,17920]{1,0:T(8,128)} fusion(bf16[256,8960]{1,0:T(8,128)(2,1)} %get-tuple-element.36, bf16[256,8960]{1,0:T(8,128)(2,1)} %get-tuple-element.35, f32[256,1536]{1,0:T(8,128)S(1)} %get-tuple-element.117, f32[1536]{0:T(1024)S(1)} %reshape.720, f32[256]{0:T(256)S(1)} %add_rsqrt_fusion.1), kind=kOutput, calls=%fused_computation.8 | convolution fusion | flops 14112391168 | bytes 120855552 | tf_op jit(solution)/shard_map/nc,nk->ck/dot_general | solution.py:290
  1351.1 5.9 multiply_convert_fusion.3
  1363.9 24.9 convolution_bitcast_fusion
  1388.7 6.2 fusion.294
  1419.1 6.2 all-to-all-done.5
  1427.8 8.1 fusion.363
  1436.0 119.1 %pad_maximum_fusion = f32[1536,30464]{1,0:T(8,128)} fusion(f32[1536,8960]{1,0:T(8,128)} %convolution_bitcast_fusion, f32[1536,17920]{1,0:T(8,128)} %fusion.1, f32[1536,1536]{1,0:T(8,128)S(1)} %bitcast.907, f32[1536,2048]{1,0:T(8,128)} %fusion.363), kind=kLoop, calls=%fused_computation | loop fusion | flops 140378112 | bytes 374341632 | tf_op jit(solution)/shard_map/concatenate | solution.py:284
  1555.5 1513.3 %reduce-scatter.5.cloned.1.call-done = f32[48,30464]{1,0:T(8,128)} async-done(((f32[1536,30464]{1,0:T(8,128)}), f32[48,30464]{1,0:T(8,128)}) %reduce-scatter.5.cloned.1.call-update) | async-done | bytes 5849104 | tf_op jit(solution)/shard_map/reduce_scatter | solution.py:283
  3075.4 16.1 fusion.51
  3091.8 6.2 multiply_reduce_fusion.1
  3098.0 40.6 %all-reduce.6 = (bf16[2048]{0:T(1024)(128)(2,1)S(1)}, bf16[1536]{0:T(1024)(128)(2,1)S(1)}, bf16[1536]{0:T(1024)(128)(2,1)S(1)}) all-reduce(f32[2048]{0:T(1024)S(1)} %convert_reduce_fusion, f32[1536]{0:T(1024)S(1)} %get-tuple-element.11, f32[1536]{0:T(1024)S(1)} %copy-done.70), channel_id=5, replica_groups=mesh['wide'=2,'blk'=4,'head'=4] {'wide','blk','head'}, use_global_device_ids=true, to_apply=%region_26.27.clone | all-reduce | flops 5120 | bytes 30720
  3139.4 32.9 all-reduce.7
  3176.8 128.5 %all-gather.20.cloned.1.call-done = bf16[768,30464]{1,0:T(8,128)(2,1)} async-done(((bf16[48,30464]{1,0:T(8,128)(2,1)}), bf16[768,30464]{1,0:T(8,128)(2,1)}) %all-gather.20.cloned.1.call-update) | async-done | bytes 46792720 | tf_op jit(solution)/shard_map/all_gather | solution.py:307
  3315.2 15.5 slice.336
  3330.7 26.0 slice.335
  (385 shorter events, 248.6 us)
Async XLA Ops:
  7.2 85.5 %all-gather.10.cloned.1.call-start = ((), (), s32[]{:S(2)}) async-start(), calls=%async_computation.8 | async-start | bytes 9437184 | tf_op jit(solution)/shard_map/all_gather | solution.py:85
  8.0 147.2 %all-gather.12.cloned.1.call-start = ((), (), s32[]{:S(2)}) async-start(), calls=%async_computation.9 | async-start | bytes 2621440 | tf_op jit(solution)/shard_map/all_gather | solution.py:133
  8.7 88.6 %copy-start.68 = (f32[256]{0:T(256)}, f32[256]{0:T(256)S(1)}, u32[]{:S(2)}) copy-start(f32[256]{0:T(256)S(1)} %rsqrt.20) | copy-start | bytes 3076
  14.0 83.3 %copy-start.62 = (f32[1536]{0:T(1024)}, f32[1536]{0:T(1024)S(1)}, u32[]{:S(2)}) copy-start(f32[1536]{0:T(1024)S(1)} %reshape.719) | copy-start | bytes 18436
  19.0 92.9 %copy-start.30 = (f32[256,128]{1,0:T(8,128)}, f32[256,128]{1,0:T(8,128)S(1)}, u32[]{:S(2)}) copy-start(f32[256,128]{1,0:T(8,128)S(1)} %get-tuple-element.55) | copy-start | bytes 393220
  19.0 117.5 %copy-start.13 = (f32[256,128]{1,0:T(8,128)}, f32[256,128]{1,0:T(8,128)S(1)}, u32[]{:S(2)}) copy-start(f32[256,128]{1,0:T(8,128)S(1)} %get-tuple-element.54) | copy-start | bytes 393220
  19.3 78.0 %copy-start.12 = (bf16[256,1536]{1,0:T(8,128)(2,1)}, bf16[256,1536]{1,0:T(8,128)(2,1)S(1)}, u32[]{:S(2)}) copy-start(bf16[256,1536]{1,0:T(8,128)(2,1)S(1)} %multiply_convert_fusion.5) | copy-start | bytes 2359300
  110.0 108.1 %all-gather.14.cloned.1.call-start = ((), (), s32[]{:S(2)}) async-start(), calls=%async_computation.10 | async-start | bytes 7077888 | tf_op jit(solution)/shard_map/all_gather | solution.py:86
  110.7 741.4 %all-gather.16.cloned.1.call-start = ((), (), s32[]{:S(2)}) async-start(), calls=%async_computation.11 | async-start | bytes 82575360 | tf_op jit(solution)/shard_map/all_gather | solution.py:87
  111.3 1064.3 %all-gather.18.cloned.1.call-start = ((), (), s32[]{:S(2)}) async-start(), calls=%async_computation.12 | async-start | bytes 41287680 | tf_op jit(solution)/shard_map/all_gather | solution.py:88
  132.2 15.3 all-to-all-start.1
  183.5 30.2 all-to-all-start.2
  222.0 1020.5 %copy-start.8 = (f32[256,1536]{1,0:T(8,128)}, f32[256,1536]{1,0:T(8,128)S(1)}, u32[]{:S(2)}) copy-start(f32[256,1536]{1,0:T(8,128)S(1)} %get-tuple-element.117) | copy-start | bytes 4718596
  852.1 323.5 %copy-start.15 = (bf16[2,2,64,1536]{3,2,1,0:T(8,128)(2,1)S(1)}, bf16[2,2,64,1536]{3,2,1,0:T(8,128)(2,1)}, u32[]{:S(2)}) copy-start(bf16[2,2,64,1536]{3,2,1,0:T(8,128)(2,1)} %param.21) | copy-start | bytes 2359300
  1228.5 160.2 %copy-start = (f32[256,1536]{1,0:T(8,128)}, f32[256,1536]{1,0:T(8,128)S(1)}, u32[]{:S(2)}) copy-start(f32[256,1536]{1,0:T(8,128)S(1)} %multiply_add_fusion) | copy-start | bytes 4718596
  1238.3 44.7 %all-to-all-start.3 = ((bf16[2,2,64,4,384]{4,2,1,0,3:T(8,128)(2,1)}), bf16[2,2,64,4,384]{4,2,1,0,3:T(8,128)(2,1)}, u32[]{:S(2)}, u32[]{:S(2)}) async-start(bf16[2,2,64,4,384]{4,2,1,0,3:T(8,128)(2,1)} %copy.646), calls=%async_computation.3 | async-start | bytes 1572864 | tf_op jit(solution)/shard_map/all_to_all | solution.py:205
  1242.5 167.6 %reduce-scatter.3.cloned.1.call-start = ((), (), s32[]{:S(2)}) async-start(), calls=%async_computation.13 | async-start | bytes 2621440 | tf_op jit(solution)/shard_map/reduce_scatter | solution.py:249
  1360.1 34.8 %all-to-all-start.4 = ((bf16[2,2,256,1,384]{4,1,0,3,2:T(2,128)(2,1)}), bf16[2,2,256,1,384]{4,1,0,3,2:T(2,128)(2,1)S(1)}, u32[]{:S(2)}, u32[]{:S(2)}) async-start(bf16[2,2,256,1,384]{4,1,0,3,2:T(2,128)(2,1)} %copy.694), calls=%async_computation.4 | async-start | bytes 1572864 | tf_op jit(solution)/shard_map/all_to_all | solution.py:254
  1412.2 13.1 all-to-all-start.5
  1416.4 1652.4 %reduce-scatter.5.cloned.1.call-start = ((), (), s32[]{:S(2)}) async-start(), calls=%async_computation.14 | async-start | bytes 193019904 | tf_op jit(solution)/shard_map/reduce_scatter | solution.py:283
  1555.2 1518.3 %copy-start.75 = (u32[32]{0:T(128)S(1)}, u32[32]{0:T(128)}, u32[]{:S(2)}) copy-start(u32[32]{0:T(128)} %constant.43) | copy-start | bytes 388
  1555.2 1520.1 %copy-start.9 = (f32[256,1536]{1,0:T(8,128)S(1)}, f32[256,1536]{1,0:T(8,128)}, u32[]{:S(2)}) copy-start(f32[256,1536]{1,0:T(8,128)} %copy-done.8) | copy-start | bytes 4718596
  1555.2 1750.1 %all-gather.20.cloned.1.call-start = ((), (), s32[]{:S(2)}) async-start(), calls=%async_computation.15 | async-start | bytes 49717248 | tf_op jit(solution)/shard_map/all_gather | solution.py:307
  3091.7 82.3 %copy-start.1 = (f32[256,1536]{1,0:T(8,128)S(1)}, f32[256,1536]{1,0:T(8,128)}, u32[]{:S(2)}) copy-start(f32[256,1536]{1,0:T(8,128)} %copy-done) | copy-start | bytes 4718596
  (77 other events, 720.3 us)
Sparse Core Ops, SparseCore 0:
  9.6 83.0 all-gather.9
  110.1 45.0 all-gather.11
  156.7 61.3 all-gather.13
  219.6 632.5 all-gather.15
  853.5 322.0 all-gather.17
  1351.2 44.3 reduce-scatter.2
  1555.3 1513.5 reduce-scatter.4
  3073.5 231.7 all-gather.19
where the time goes:
time: 3370 us; the launch traced here: 3360 us
  waiting for transfers between devices  2650 us (79%)
  matrix products  305 us (9%)
  other arithmetic  163 us (5%)
  local copies, waits for them, and re-layouts  107 us (3%)
  blocking collectives  98.8 us (3%)
    reduce_scatter x1, waiting for transfers between devices, on_device(): lax.psum_scatter(jnp.concatenate([jnp.einsum('nc,nk->ck', normed_attn, gr...  1510 us
    all_gather x1, waiting for transfers between devices, on_device(): lax.all_gather(w_gate_up, 'wide', axis=0, tiled=True)  630 us
    all_gather x1, waiting for transfers between devices, on_device(): lax.all_gather(w_down, 'wide', axis=0, tiled=True)  286 us
    all_gather x1, waiting for transfers between devices, on_device(): lax.all_gather(part_rows[None].astype(jnp.bfloat16), ('blk', 'head'), axi...  128 us
    concatenate x1, other arithmetic, on_device(): jnp.concatenate([jnp.einsum('nc,nk->ck', normed_attn, grad_projected, pre...  119 us
    unnamed x2, blocking collectives  73.5 us
    all_gather x1, waiting for transfers between devices, on_device(): lax.all_gather(w_qkv, 'wide', axis=0, tiled=True)  73.4 us
  transfers between devices with their start and end apart: 13, of which 9 were waited for; matrix products, arithmetic and copies ran while one was open for 7% of the time, Pallas kernels for 0%

commit v1 on v0

v1 whole, which is shorter than its diff:
```python
import jax
import jax.numpy as jnp
from jax import lax
from jax.sharding import Mesh, PartitionSpec as P

QUERY_HEADS = 12
KEY_VALUE_HEADS = 2
HEAD_SIZE = 128
LANES = 128

norm_eps = 1e-06
rope_theta = 1000000.0
masked_score = -1e30

WIDE = ("wh", "wl")
GROUP = ("wl", "blk", "core")
PLANE = ("blk", "hx", "core")
f32, bf16 = jnp.float32, jnp.bfloat16


def rms_parts(values, gain_row):
    inverse = lax.rsqrt(jnp.mean(values * values, axis=-1, keepdims=True) + norm_eps)
    scaled = values * inverse
    return (scaled * gain_row, scaled, inverse)


def rms_back(grad_normed, scaled, inverse, gain_row):
    grad_scaled = grad_normed * gain_row
    mean_term = jnp.mean(grad_scaled * scaled, axis=-1, keepdims=True)
    return (inverse * (grad_scaled - scaled * mean_term), jnp.sum(grad_normed * scaled, axis=0))


def half_turn(values):
    half_size = values.shape[-1] // 2
    return jnp.concatenate([-values[..., half_size:], values[..., :half_size]], axis=-1)


def rotate_pairs(values, cosine_table, sine_values):
    return values * cosine_table + half_turn(values) * sine_values


def turn_back(values, cosine_table, sine_values):
    return values * cosine_table - half_turn(values * sine_values)


def rope_tables(positions):
    frequency = rope_theta ** (-jnp.arange(0, HEAD_SIZE, 2).astype(f32) / HEAD_SIZE)
    angles = positions.astype(f32)[:, None] * frequency[None, :]
    angles = jnp.concatenate([angles, angles], axis=-1)
    return (jnp.cos(angles), jnp.sin(angles))


def dot(a, b):
    return jnp.dot(a, b, preferred_element_type=f32)


def dot_rows(a, b):
    return lax.dot_general(a, b, (((0,), (0,)), ((), ())), preferred_element_type=f32)


def dot_cols(a, b):
    return lax.dot_general(a, b, (((1,), (1,)), ((), ())), preferred_element_type=f32)


def partner(values, axis, distance=1):
    count = lax.axis_size(axis)
    return lax.ppermute(values, axis, [(i, i ^ distance) for i in range(count)])


def shifted(values, axis, distance):
    count = lax.axis_size(axis)
    return lax.ppermute(values, axis, [((i + distance) % count, i) for i in range(count)])


def in_order(pieces, index):
    bit = 1
    while bit < len(pieces):
        odd = (index & bit) != 0
        pieces = [jnp.where(odd, pieces[k ^ bit], pieces[k]) for k in range(len(pieces))]
        bit *= 2
    return pieces


def gather_wide(own_by_parity, wide_index):
    count = lax.axis_size(WIDE)
    pieces = [own_by_parity[0]]
    for distance in range(1, count):
        pieces.append(partner(own_by_parity[(distance & 1) % len(own_by_parity)], WIDE, distance))
    return jnp.concatenate(in_order(pieces, wide_index), axis=0)


def on_device(
    tokens,
    positions,
    block_order,
    w_qkv,
    qkv_bias,
    w_out,
    w_gate_up,
    w_down,
    gain_attn,
    gain_mlp,
    cotangent,
):
    slot_count, seq_count, rows_dev, width = tokens.shape
    blk_count, x_count, core_count = (lax.axis_size(a) for a in ("blk", "hx", "core"))
    wide_count = lax.axis_size(WIDE)
    wide_at, wl_at, blk_at, x_at, core_at = (
        lax.axis_index(a) for a in (WIDE, "wl", "blk", "hx", "core")
    )
    head_at = x_at * core_count + core_at
    head_shards = x_count * core_count
    q_here = QUERY_HEADS // head_shards * HEAD_SIZE
    heads_here = QUERY_HEADS // head_shards
    q_total = QUERY_HEADS * HEAD_SIZE
    kv_total = KEY_VALUE_HEADS * HEAD_SIZE
    kv_at = head_at * KEY_VALUE_HEADS // head_shards
    rows_wide = w_qkv.shape[0]
    block_rows = rows_dev * head_shards
    dev_rows = slot_count * seq_count * rows_dev
    blk_rows = dev_rows * head_shards
    ff = w_down.shape[1]
    score_scale = HEAD_SIZE ** (-0.5)

    def gather_head(values):
        pair = jnp.stack([values, partner(values, "hx")])
        other = partner(pair, "core")
        return jnp.stack(in_order([pair, other], core_at))

    def block_major(values):
        return jnp.moveaxis(values, (0, 1), (2, 3))

    small = jnp.concatenate([qkv_bias, gain_attn, gain_mlp])[None]
    small = gather_wide([small], wide_at)
    bias_len = qkv_bias.shape[0]
    bias_row = small[:, :bias_len].reshape(1, -1).astype(f32)
    gain_attn_row = small[:, bias_len : bias_len + rows_wide].reshape(1, -1).astype(f32)
    gain_mlp_row = small[:, bias_len + rows_wide :].reshape(1, -1).astype(f32)

    def head_columns(array):
        return jnp.concatenate(
            [
                lax.dynamic_slice_in_dim(array, head_at * q_here, q_here, 1),
                lax.dynamic_slice_in_dim(array, q_total + kv_at * HEAD_SIZE, HEAD_SIZE, 1),
                lax.dynamic_slice_in_dim(
                    array, q_total + kv_total + kv_at * HEAD_SIZE, HEAD_SIZE, 1
                ),
            ],
            axis=1,
        )

    w_head = gather_wide([head_columns(w_qkv)], wide_at)
    bias_head = head_columns(bias_row)

    share = 2 * blk_count * core_count
    main = ff // (LANES * share) * LANES
    rest = ff // share - main

    def ff_columns(parity):
        at = ((wl_at ^ parity) * blk_count + blk_at) * core_count + core_at
        gate_main, rest_main = at * main, share * main + at * rest
        down = [
            lax.dynamic_slice_in_dim(w_down, gate_main, main, 1),
            lax.dynamic_slice_in_dim(w_down, rest_main, rest, 1),
        ]
        gate_up = [
            lax.dynamic_slice_in_dim(w_gate_up, gate_main, main, 1),
            lax.dynamic_slice_in_dim(w_gate_up, ff + gate_main, main, 1),
            lax.dynamic_slice_in_dim(w_gate_up, rest_main, rest, 1),
            lax.dynamic_slice_in_dim(w_gate_up, ff + rest_main, rest, 1),
        ]
        return jnp.concatenate(down + gate_up, axis=1)

    flat_tokens = tokens.reshape(-1, width)
    blk_tokens = block_major(gather_head(tokens)).reshape(-1, width)
    blk_positions = block_major(gather_head(positions)).reshape(-1)
    w_out_half = lax.dynamic_slice_in_dim(
        w_out, core_at * (rows_wide // 2), rows_wide // 2, 0
    )
    out_pieces = [w_out]
    for distance in range(1, wide_count):
        mine = partner(w_out_half, WIDE, distance)
        out_pieces.append(
            jnp.concatenate(in_order([mine, partner(mine, "core")], core_at), axis=0)
        )
    full_out = jnp.concatenate(in_order(out_pieces, wide_at), axis=0)
    w_out_head = lax.dynamic_slice_in_dim(full_out, head_at * q_here, q_here, 1)

    w_ff = gather_wide([ff_columns(0), ff_columns(1)], wide_at)
    w_down_here = w_ff[:, : main + rest]
    w_gate_up_here = w_ff[:, main + rest :]

    group_cotangent = lax.all_gather(
        cotangent.reshape(-1, width), GROUP, axis=0, tiled=True
    )

    normed_attn = rms_parts(blk_tokens.astype(f32), gain_attn_row)[0].astype(bf16)
    projected = dot(normed_attn, w_head) + bias_head
    cosine_table, sine_values = rope_tables(blk_positions)
    queries = (
        rotate_pairs(
            projected[:, :q_here].reshape(-1, heads_here, HEAD_SIZE),
            cosine_table[:, None, :],
            sine_values[:, None, :],
        )
        .astype(bf16)
        .reshape(slot_count, seq_count, block_rows, heads_here, HEAD_SIZE)
    )
    keys = rotate_pairs(projected[:, q_here : q_here + HEAD_SIZE], cosine_table, sine_values)
    pair = [keys.astype(bf16), projected[:, q_here + HEAD_SIZE :].astype(bf16)]
    sent = jnp.where(core_at == 0, pair[0], pair[1])
    arrived = jnp.stack([shifted(sent, "blk", d) for d in range(1, blk_count)])
    other = partner(arrived, "core")
    kv_shape = (blk_count * slot_count, seq_count, block_rows, HEAD_SIZE)
    all_keys, all_values = (
        jnp.concatenate([own[None], far]).reshape(kv_shape)
        for own, far in zip(pair, in_order([arrived, other], core_at))
    )
    key_slots = (
        (blk_at + jnp.arange(blk_count, dtype=jnp.int32)) % blk_count * slot_count
    )[:, None] + jnp.arange(slot_count, dtype=jnp.int32)[None]
    key_order = jnp.take(block_order, key_slots.reshape(-1))
    query_order = key_order[:slot_count]
    row_ids = (
        (2 * (jnp.arange(2, dtype=jnp.int32) ^ x_at))[None, :, None]
        + jnp.arange(2, dtype=jnp.int32)[:, None, None]
    ) * rows_dev + jnp.arange(rows_dev, dtype=jnp.int32)[None, None]
    row_ids = row_ids.reshape(-1)
    allowed = (key_order[None, :] < query_order[:, None])[:, None, None, :, None] | (
        (key_order[None, :] == query_order[:, None])[:, None, None, :, None]
        & (row_ids[None, :] <= row_ids[:, None])[None, :, None, None, :]
    )
    allowed = allowed[:, None]
    scores = (
        jnp.einsum("asrhd,kscd->asrhkc", queries, all_keys, preferred_element_type=f32)
        * score_scale
    )
    masked = jnp.where(allowed, scores, masked_score)
    peak = jnp.max(masked, axis=(-2, -1), keepdims=True)
    weights = jnp.exp(masked - peak)
    total = jnp.sum(weights, axis=(-2, -1), keepdims=True)
    log_total = peak + jnp.log(total)
    attention = jnp.einsum(
        "asrhkc,kscd->asrhd",
        (weights / total).astype(bf16),
        all_values,
        preferred_element_type=f32,
    )
    attended_head = attention.astype(bf16).reshape(blk_rows, q_here)

    back = attended_head.reshape(slot_count, seq_count, 2, 2, rows_dev, q_here)
    from_x = partner(back[:, :, :, 1], "hx")
    by_x = jnp.stack([back[:, :, :, 0], from_x])
    own_c, other_c = in_order([by_x[:, :, :, 0], by_x[:, :, :, 1]], core_at)
    by_core = in_order([own_c, partner(other_c, "core")], core_at)
    by_head = [
        piece for x_piece in zip(*(in_order(list(p), x_at) for p in by_core)) for piece in x_piece
    ]
    attended = jnp.concatenate(by_head, axis=-1).reshape(dev_rows, q_total)
    middle = flat_tokens.astype(f32) + dot_cols(attended, full_out)
    normed_mlp, scaled_mlp, inverse_mlp = rms_parts(middle, gain_mlp_row)
    normed_mlp = normed_mlp.astype(bf16)

    group_normed = lax.all_gather(normed_mlp, GROUP, axis=0, tiled=True)
    grad_hidden = dot(group_cotangent, w_down_here)
    gate_up = dot(group_normed, w_gate_up_here)

    def parts(values):
        return (
            (values[:, :main], values[:, main : 2 * main]),
            (values[:, 2 * main : 2 * main + rest], values[:, 2 * main + rest :]),
        )

    def gated(gate, up, grad):
        sigmoid = jax.nn.sigmoid(gate)
        silu = gate * sigmoid
        return (
            (silu * up).astype(bf16),
            (grad * up * sigmoid * (1.0 + gate * (1.0 - sigmoid))).astype(bf16),
            (grad * silu).astype(bf16),
        )

    (gate_m, up_m), (gate_r, up_r) = parts(gate_up)
    hidden_m, gg_m, gu_m = gated(gate_m, up_m, grad_hidden[:, :main])
    hidden_r, gg_r, gu_r = gated(gate_r, up_r, grad_hidden[:, main:])
    hidden = jnp.concatenate([hidden_m, hidden_r], axis=1)
    grad_gate_up = jnp.concatenate([gg_m, gu_m, gg_r, gu_r], axis=1)
    grad_normed_part = dot_cols(grad_gate_up, w_gate_up_here).astype(bf16)
    mlp_part = dot_cols(hidden, w_down_here).astype(bf16)
    grad_normed_mlp = lax.psum_scatter(
        grad_normed_part, GROUP, scatter_dimension=0, tiled=True
    ).astype(f32)

    ff_grad = jnp.concatenate(
        [dot_rows(group_cotangent, hidden), dot_rows(group_normed, grad_gate_up)], axis=1
    ).astype(bf16)
    half = rows_wide // 2
    halves = ff_grad.reshape(wide_count, 2, half, -1)
    mine, theirs = in_order([halves[:, 0], halves[:, 1]], x_at)
    ff_sum = mine.astype(f32) + partner(theirs, "hx").astype(f32)
    ff_send = ff_sum.astype(bf16)
    by_parity = [None, None]
    for distance in range(wide_count):
        rows_of = lax.dynamic_index_in_dim(ff_send, wide_at ^ distance, 0, keepdims=False)
        term = rows_of if distance == 0 else partner(rows_of, WIDE, distance)
        term = term.astype(f32)
        kept = by_parity[distance & 1]
        by_parity[distance & 1] = term if kept is None else kept + term
    ff_done = jnp.stack(in_order(by_parity, wl_at)).astype(bf16)
    ff_all = lax.all_gather(ff_done, PLANE, axis=0)
    ff_all = ff_all.reshape(blk_count, x_count, core_count, 2, half, -1)

    mlp_out = lax.psum_scatter(mlp_part, GROUP, scatter_dimension=0, tiled=True).astype(f32)
    output = (middle + mlp_out).astype(bf16).reshape(tokens.shape)

    grad_middle_part, grad_gain_mlp = rms_back(
        grad_normed_mlp, scaled_mlp, inverse_mlp, gain_mlp_row
    )
    grad_middle = cotangent.reshape(-1, width).astype(f32) + grad_middle_part
    grad_branch = grad_middle.astype(bf16)
    blk_branch = block_major(gather_head(grad_branch.reshape(tokens.shape))).reshape(-1, width)
    out_grad_part = dot_rows(blk_branch, attended_head)
    grad_heads = (
        dot(blk_branch, w_out_head)
        .astype(bf16)
        .reshape(slot_count, seq_count, block_rows, heads_here, HEAD_SIZE)
    )
    row_inner = jnp.sum(grad_heads.astype(f32) * attention, axis=-1)
    probs = jnp.exp(masked - log_total)
    grad_probs = jnp.einsum(
        "asrhd,kscd->asrhkc", grad_heads, all_values, preferred_element_type=f32
    )
    grad_scores = (probs * (grad_probs - row_inner[..., None, None])).astype(bf16)
    grad_queries = (
        jnp.einsum("asrhkc,kscd->asrhd", grad_scores, all_keys, preferred_element_type=f32)
        * score_scale
    )
    grad_keys = (
        jnp.einsum("asrhkc,asrhd->kscd", grad_scores, queries, preferred_element_type=f32)
        * score_scale
    )
    grad_values = jnp.einsum(
        "asrhkc,asrhd->kscd", probs.astype(bf16), grad_heads, preferred_element_type=f32
    )
    kept, given = in_order([grad_keys, grad_values], core_at)
    kept = kept + partner(given.astype(bf16), "core").astype(f32)
    kept = kept.reshape(blk_count, blk_rows, HEAD_SIZE)
    grad_pair = kept[0]
    for distance in range(1, blk_count):
        grad_pair = grad_pair + shifted(
            kept[blk_count - distance].astype(bf16), "blk", distance
        ).astype(f32)
    grad_pair = jnp.where(
        core_at == 0, turn_back(grad_pair, cosine_table, sine_values), grad_pair
    )
    grad_projected = jnp.concatenate(
        [
            turn_back(
                grad_queries.reshape(-1, heads_here, HEAD_SIZE),
                cosine_table[:, None, :],
                sine_values[:, None, :],
            ).reshape(-1, q_here),
            grad_pair,
        ],
        axis=1,
    ).astype(bf16)
    w_back = jnp.concatenate(
        [
            w_head[:, :q_here],
            jnp.where(
                core_at == 0,
                w_head[:, q_here : q_here + HEAD_SIZE],
                w_head[:, q_here + HEAD_SIZE :],
            ),
        ],
        axis=1,
    )
    back_part = dot_cols(grad_projected, w_back).astype(bf16)
    back_part = back_part.reshape(slot_count, seq_count, 2, 2, rows_dev, width)
    own_c, other_c = in_order([back_part[:, :, 0], back_part[:, :, 1]], core_at)
    own_c = own_c.astype(f32) + partner(other_c, "core").astype(f32)
    grad_normed_attn = own_c[:, :, 0] + partner(own_c[:, :, 1].astype(bf16), "hx").astype(f32)
    grad_normed_attn = grad_normed_attn.reshape(-1, width)
    scaled_attn, inverse_attn = rms_parts(flat_tokens.astype(f32), gain_attn_row)[1:]
    grad_flat, grad_gain_attn = rms_back(
        grad_normed_attn, scaled_attn, inverse_attn, gain_attn_row
    )
    input_grad = (grad_middle + grad_flat).astype(bf16).reshape(tokens.shape)

    column_sums = jnp.sum(grad_projected.astype(f32), axis=0)
    bias_sum = jnp.zeros((q_total + 2 * kv_total,), f32)
    bias_sum = lax.dynamic_update_slice(bias_sum, column_sums[:q_here], (head_at * q_here,))
    bias_sum = lax.dynamic_update_slice(
        bias_sum,
        column_sums[q_here:],
        (q_total + core_at * kv_total + kv_at * HEAD_SIZE,),
    )
    sums = jnp.concatenate([bias_sum, grad_gain_attn, grad_gain_mlp]).reshape(-1, LANES)
    for axis in ("core", "hx", "blk", "wl", "wh"):
        step = 1
        while step < lax.axis_size(axis):
            sums = sums + partner(sums, axis, step)
            step *= 2
    sums = sums.reshape(-1)
    bias_at = q_total + 2 * kv_total
    bias_grad = lax.dynamic_slice_in_dim(sums, wide_at * bias_len, bias_len)
    gain_attn_grad = lax.dynamic_slice_in_dim(sums, bias_at + wide_at * rows_wide, rows_wide)
    gain_mlp_grad = lax.dynamic_slice_in_dim(
        sums, bias_at + width + wide_at * rows_wide, rows_wide
    )

    proj_part = jnp.concatenate(
        [dot_rows(normed_attn, grad_projected), out_grad_part], axis=1
    ).astype(bf16)
    proj_done = lax.psum_scatter(
        proj_part, WIDE + ("blk",), scatter_dimension=0, tiled=True
    )
    proj_all = lax.all_gather(proj_done, PLANE, axis=0)
    proj_all = proj_all.reshape(blk_count, x_count, core_count, rows_wide // blk_count, -1)
    proj_q = proj_all[..., :q_here].transpose(0, 3, 1, 2, 4).reshape(rows_wide, q_total)
    proj_kv = proj_all[..., q_here : q_here + HEAD_SIZE]
    proj_kv = proj_kv.transpose(0, 3, 2, 1, 4).reshape(rows_wide, 2 * kv_total)
    proj_o = proj_all[..., q_here + HEAD_SIZE :].transpose(0, 3, 1, 2, 4)
    qkv_grad = jnp.concatenate([proj_q, proj_kv], axis=1).astype(f32)
    out_grad = proj_o.reshape(rows_wide, q_total).astype(f32)

    def columns(first, size):
        piece = ff_all[..., first : first + size]
        return piece.transpose(1, 4, 3, 0, 2, 5).reshape(rows_wide, share * size)

    at = main + rest
    down_grad = jnp.concatenate([columns(0, main), columns(main, rest)], axis=1).astype(f32)
    gate_up_grad = jnp.concatenate(
        [
            columns(at, main),
            columns(at + 2 * main, rest),
            columns(at + main, main),
            columns(at + 2 * main + rest, rest),
        ],
        axis=1,
    ).astype(f32)
    return (
        output,
        input_grad,
        qkv_grad,
        bias_grad,
        out_grad,
        gate_up_grad,
        down_grad,
        gain_attn_grad,
        gain_mlp_grad,
    )


def solution(mesh):
    wide, blk, head = mesh.devices.shape
    cores = 2
    fine = Mesh(
        mesh.devices.reshape(wide // 2, 2, blk, head // cores, cores),
        ("wh", "wl", "blk", "hx", "core"),
    )
    rows = P("blk", WIDE, ("hx", "core"), None)
    matrix, vector = P(WIDE, None), P(WIDE)
    in_specs = (
        rows,
        P("blk", WIDE, ("hx", "core")),
        P(),
        matrix,
        vector,
        matrix,
        matrix,
        matrix,
        vector,
        vector,
        rows,
    )
    out_specs = (rows, rows, matrix, vector, matrix, matrix, matrix, vector, vector)
    return jax.shard_map(
        on_device, mesh=fine, in_specs=in_specs, out_specs=out_specs, check_vma=False
    )
```

time: 3370 us -> 1400 us (0.42)
  waiting for transfers between devices: 2650 us -> 667 us
  local copies, waits for them, and re-layouts: 107 us -> 321 us
  matrix products: 305 us -> 187 us
  blocking collectives: 98.8 us -> 0 us
    reduce_scatter x2 -> x3, waiting for transfers between devices: 1510 us -> 181 us  [the longest x1 135 us: on_device(): lax.psum_scatter(grad_normed_part, GROUP, scatter_dimension=0, tiled=True)]
    all_gather x6 -> x4, waiting for transfers between devices: 1130 us -> 197 us  [the longest x1 173 us: on_device(): ff_all = lax.all_gather(ff_done, PLANE, axis=0)]
    ppermute x0 -> x30, waiting for transfers between devices: none -> 289 us  [the longest x24 255 us: partner(): return lax.ppermute(values, axis, [(i, i ^ distance) for i in range(count)])]
    transpose x0 -> x8, local copies, waits for them, and re-layouts: none -> 123 us  [the longest x4 118 us: columns(): return piece.transpose(1, 4, 3, 0, 2, 5).reshape(rows_wide, share * size)]
    dot_general x68 -> x18, matrix products: 305 us -> 187 us  [the longest x4 42.3 us: dot_rows(): lax.dot_general(a, b, (((0,), (0,)), ((), ())), preferred_element_type=f32)]
    concatenate x2 -> x7, other arithmetic: 119 us -> 3.1 us  [the longest x2 1.74 us: head_columns(): jnp.concatenate([lax.dynamic_slice_in_dim(array, head_at * q_here, q_here...]
    unnamed x2 -> x0, blocking collectives: 73.5 us -> none
    convert_element_type x13 -> x16, other arithmetic: 12.6 us -> 85.4 us  [the longest x1 26.4 us: on_device(): gate_up_grad = jnp.concatenate([columns(at, main), columns(at + 2 * main,...]
  transfers between devices with their start and end apart: 13 -> 37, of which waited for: 9 -> 24; matrix products, arithmetic and copies ran while one was open for 7% -> 21% of each run, Pallas kernels for 0% -> 0%
where the time goes in v1:
time: 1400 us; the launch traced here: 1390 us
  waiting for transfers between devices  667 us (48%)
  local copies, waits for them, and re-layouts  321 us (23%)
  matrix products  187 us (13%)
  other arithmetic  164 us (12%)
  starting transfers between devices  36.2 us (3%)
  between operations  16.3 us (1%)
    ppermute x24, waiting for transfers between devices, partner(): return lax.ppermute(values, axis, [(i, i ^ distance) for i in range(count)])  255 us
    all_gather x1, waiting for transfers between devices, on_device(): ff_all = lax.all_gather(ff_done, PLANE, axis=0)  173 us
    reduce_scatter x1, waiting for transfers between devices, on_device(): lax.psum_scatter(grad_normed_part, GROUP, scatter_dimension=0, tiled=True)  135 us
    transpose x4, local copies, waits for them, and re-layouts, columns(): return piece.transpose(1, 4, 3, 0, 2, 5).reshape(rows_wide, share * size)  118 us
    reshape x6, local copies, waits for them, and re-layouts, columns(): return piece.transpose(1, 4, 3, 0, 2, 5).reshape(rows_wide, share * size)  66.1 us
    unnamed x217, local copies, waits for them, and re-layouts  47.1 us
    reduce_scatter x1, waiting for transfers between devices, on_device(): lax.psum_scatter(proj_part, WIDE + ('blk',), scatter_dimension=0, tiled=T...  46 us
    dot_general x4, matrix products, dot_rows(): lax.dot_general(a, b, (((0,), (0,)), ((), ())), preferred_element_type=f32)  42.3 us
  transfers between devices with their start and end apart: 37, of which 24 were waited for; matrix products, arithmetic and copies ran while one was open for 21% of the time, Pallas kernels for 0%

profile of v1, /device:TPU:0, one launch (start us, length us, event | category | flops | bytes accessed | tf_op | source)
XLA Modules:
  0.0 1391.4 jit_solution(15049849239746373449)
XLA Ops:
  81.6 16.7 %collective-permute-done.7 = bf16[1024,128]{0,1:T(8,128)(2,1)S(1)} collective-permute-done((bf16[1024,128]{0,1:T(8,128)(2,1)S(1)}, bf16[1024,128]{0,1:T(8,128)(2,1)S(1)}, u32[]{:S(2)}, u32[]{:S(2)}) %collective-permute-start.7) | collective-permute-done | bytes 262176 | tf_op jit(solution)/shard_map/ppermute | solution.py:72
  206.4 82.6 %collective-permute-done.14 = bf16[768,1680]{0,1:T(8,128)(2,1)} collective-permute-done((bf16[768,1680]{0,1:T(8,128)(2,1)}, bf16[768,1680]{0,1:T(8,128)(2,1)}, u32[]{:S(2)}, u32[]{:S(2)}) %collective-permute-start.14) | collective-permute-done | bytes 2580512 | tf_op jit(solution)/shard_map/ppermute | solution.py:67
  306.5 20.4 %all-gather.6.cloned.1.call-done = bf16[4096,1536]{1,0:T(8,128)(2,1)} async-done(((bf16[256,1536]{1,0:T(8,128)(2,1)}), bf16[4096,1536]{1,0:T(8,128)(2,1)}) %all-gather.6.cloned.1.call-update) | async-done | bytes 12582928 | tf_op jit(solution)/shard_map/all_gather | solution.py:264
  326.9 22.1 %fusion.108 = f32[4096,1120]{0,1:T(8,128)} fusion(bf16[4096,1536]{1,0:T(8,128)(2,1)} %all-gather.6.cloned.1.call-done, bf16[768,1680]{0,1:T(8,128)(2,1)} %get-tuple-element.45, bf16[768,1680]{0,1:T(8,128)(2,1)} %get-tuple-element.44), kind=kOutput, calls=%fused_computation.306 | convolution fusion | flops 14099742720 | bytes 36093952 | tf_op jit(solution)/shard_map/dot_general | solution.py:54
  351.8 14.8 %multiply_convert_fusion.1 = (bf16[4096,512]{0,1:T(8,128)(2,1)}, bf16[4096,512]{0,1:T(8,128)(2,1)}, bf16[4096,512]{0,1:T(8,128)(2,1)}) fusion(f32[4096,560]{0,1:T(8,128)} %convolution_bitcast_fusion, f32[4096,1120]{0,1:T(8,128)} %fusion.108), kind=kLoop, calls=%fused_computation.26 | loop fusion | flops 31457280 | bytes 37748736 | tf_op jit(solution)/shard_map/convert_element_type | solution.py:279
  366.7 22.5 %convolution_convert_fusion.1 = bf16[4096,1536]{1,0:T(8,128)(2,1)} fusion(bf16[4096,48]{0,1:T(8,128)(2,1)S(1)} %get-tuple-element.27, bf16[4096,48]{0,1:T(8,128)(2,1)S(1)} %get-tuple-element.26, bf16[4096,512]{0,1:T(8,128)(2,1)} %get-tuple-element.25, bf16[4096,512]{0,1:T(8,128)(2,1)} %get-tuple-element.24, bf16[768,1680]{0,1:T(8,128)(2,1)} %get-tuple-element.45, ...), kind=kOutput, calls=%fused_computation.12 | convolution fusion | flops 14142734336 | bytes 26918912 | tf_op jit(solution)/shard_map/dot_general | solution.py:62
  389.7 134.8 %reduce-scatter.8.cloned.1.call-done = bf16[256,1536]{1,0:T(8,128)(2,1)} async-done(((bf16[4096,1536]{1,0:T(8,128)(2,1)}), bf16[256,1536]{1,0:T(8,128)(2,1)}) %reduce-scatter.8.cloned.1.call-update) | async-done | bytes 786448 | tf_op jit(solution)/shard_map/reduce_scatter | solution.py:290
  529.1 17.0 %collective-permute-done.15 = bf16[2,2,64,1536]{3,2,1,0:T(8,128)(2,1)S(1)} collective-permute-done((bf16[2,2,64,1536]{3,2,1,0:T(8,128)(2,1)S(1)}, bf16[2,2,64,1536]{3,2,1,0:T(8,128)(2,1)S(1)}, u32[]{:S(2)}, u32[]{:S(2)}) %collective-permute-start.15) | collective-permute-done | bytes 786464 | tf_op jit(solution)/shard_map/ppermute | solution.py:67
  572.6 15.8 %fusion.1 = bf16[2,2,256,3,8,256]{2,5,3,0,4,1:T(8,128)(2,1)} fusion(f32[2,8,256,2,256,3]{4,2,5,3,1,0:T(8,128)} %copy-done.3, f32[2,2,256,3]{2,3,0,1:T(4,128)S(1)} %fusion.45, f32[2,2,256,3]{2,3,0,1:T(4,128)S(1)} %log_add_fusion, pred[2,256,8,256]{1,3,0,2:T(8,128)(4,1)S(1)} %copy-done.31, bf16[8,2,256,128,1,1]{3,2,1,0,5,4:T(8,128)(2,1)} %bitcast.319, ...), kind=kOutput, calls=%fused_computation.4 | convolution fusion | flops 1648361472 | bytes 40656896 | tf_op jit(solution)/shard_map/asrhd,kscd->asrhkc/dot_general | solution.py:330
  696.0 46.0 %reduce-scatter.10.cloned.1.call-done = bf16[192,896]{1,0:T(8,128)(2,1)} async-done(((bf16[1536,896]{1,0:T(8,128)(2,1)}), bf16[192,896]{1,0:T(8,128)(2,1)}) %reduce-scatter.10.cloned.1.call-update) | async-done | bytes 344080 | tf_op jit(solution)/shard_map/reduce_scatter | solution.py:415
  742.6 25.3 %convolution_convert_fusion.2 = bf16[1536,1120]{0,1:T(8,128)(2,1)} fusion(bf16[4096,1536]{1,0:T(8,128)(2,1)} %all-gather.6.cloned.1.call-done, bf16[4096,48]{0,1:T(8,128)(2,1)S(1)} %copy-done.66, bf16[4096,48]{0,1:T(8,128)(2,1)S(1)} %copy-done.64, bf16[4096,512]{0,1:T(8,128)(2,1)} %get-tuple-element.25, bf16[4096,512]{0,1:T(8,128)(2,1)} %get-tuple-element.24), kind=kOutput, calls=%fused_computation.30 | convolution fusion | flops 14131281920 | bytes 25198592 | tf_op jit(solution)/shard_map/dot_general | solution.py:58
  781.4 55.5 %collective-permute-done.28 = bf16[2,384,1680]{1,2,0:T(8,128)(2,1)} collective-permute-done((bf16[2,384,1680]{1,2,0:T(8,128)(2,1)S(1)}, bf16[2,384,1680]{1,2,0:T(8,128)(2,1)}, u32[]{:S(2)}, u32[]{:S(2)}) %collective-permute-start.28) | collective-permute-done | bytes 2580512 | tf_op jit(solution)/shard_map/ppermute | solution.py:67
  844.0 36.0 %collective-permute-done.29 = bf16[384,1680]{0,1:T(8,128)(2,1)} collective-permute-done((bf16[384,1680]{0,1:T(8,128)(2,1)}, bf16[384,1680]{0,1:T(8,128)(2,1)}, u32[]{:S(2)}, u32[]{:S(2)}) %collective-permute-start.29) | collective-permute-done | bytes 1290272 | tf_op jit(solution)/shard_map/ppermute | solution.py:67
  897.7 19.4 %collective-permute-done.22 = bf16[2,2,64,1536]{3,2,1,0:T(8,128)(2,1)} collective-permute-done((bf16[2,2,64,1536]{3,2,1,0:T(8,128)(2,1)}, bf16[2,2,64,1536]{3,2,1,0:T(8,128)(2,1)}, u32[]{:S(2)}, u32[]{:S(2)}) %collective-permute-start.22) | collective-permute-done | bytes 786464 | tf_op jit(solution)/shard_map/ppermute | solution.py:67
  978.2 173.5 %all-gather.10.cloned.1.call-done = bf16[16,2,384,1680]{2,3,1,0:T(8,128)(2,1)} async-done(((bf16[1,2,384,1680]{2,3,1,0:T(8,128)(2,1)}), bf16[16,2,384,1680]{2,3,1,0:T(8,128)(2,1)}) %all-gather.10.cloned.1.call-update) | async-done | bytes 41287696 | tf_op jit(solution)/shard_map/all_gather | solution.py:310
  1154.1 24.7 %slice_bitcast_fusion = (bf16[2,384,2,4,2,512]{1,5,2,4,0,3:T(8,128)(2,1)}, bf16[2,384,2,4,2,512]{1,5,2,4,0,3:T(8,128)(2,1)}, bf16[2,384,2,4,2,512]{1,5,2,4,0,3:T(8,128)(2,1)}) fusion(bf16[4,2,2,2,384,1680]{4,5,3,2,1,0:T(8,128)(2,1)} %bitcast.290), kind=kLoop, calls=%fused_computation.15 | loop fusion | bytes 75497472 | tf_op jit(solution)/shard_map/transpose | solution.py:429
  1181.8 31.3 %copy.202 = bf16[2,384,2,4,2,512]{5,4,3,2,1,0:T(2,128)(2,1)} copy(bf16[2,384,2,4,2,512]{1,5,2,4,0,3:T(8,128)(2,1)} %get-tuple-element.19) | data formatting | bytes 25165824 | tf_op jit(solution)/shard_map/transpose | solution.py:429
  1213.0 21.0 %reshape.648 = bf16[768,8192]{1,0:T(8,128)(2,1)} reshape(bf16[2,384,2,4,2,512]{5,4,3,2,1,0:T(2,128)(2,1)} %copy.202) | data formatting | bytes 25165824 | tf_op jit(solution)/shard_map/reshape | solution.py:429
  1236.2 31.0 %copy.200 = bf16[2,384,2,4,2,512]{5,4,3,2,1,0:T(2,128)(2,1)} copy(bf16[2,384,2,4,2,512]{1,5,2,4,0,3:T(8,128)(2,1)} %get-tuple-element.20) | data formatting | bytes 25165824 | tf_op jit(solution)/shard_map/transpose | solution.py:429
  1267.2 21.3 %reshape.646 = bf16[768,8192]{1,0:T(8,128)(2,1)} reshape(bf16[2,384,2,4,2,512]{5,4,3,2,1,0:T(2,128)(2,1)} %copy.200) | data formatting | bytes 25165824 | tf_op jit(solution)/shard_map/reshape | solution.py:429
  1290.6 31.0 %copy.206 = bf16[2,384,2,4,2,512]{5,4,3,2,1,0:T(2,128)(2,1)} copy(bf16[2,384,2,4,2,512]{1,5,2,4,0,3:T(8,128)(2,1)} %get-tuple-element.18) | data formatting | bytes 25165824 | tf_op jit(solution)/shard_map/transpose | solution.py:429
  1321.7 21.0 %reshape.650 = bf16[768,8192]{1,0:T(8,128)(2,1)} reshape(bf16[2,384,2,4,2,512]{5,4,3,2,1,0:T(2,128)(2,1)} %copy.206) | data formatting | bytes 25165824 | tf_op jit(solution)/shard_map/reshape | solution.py:429
  1342.7 15.0 %maximum_convert_fusion.1 = f32[768,8960]{1,0:T(8,128)} fusion(bf16[768,768]{1,0:T(8,128)(2,1)S(1)} %copy.208, bf16[768,8192]{1,0:T(8,128)(2,1)} %reshape.650), kind=kLoop, calls=%fused_computation.13 | loop fusion | flops 27525120 | bytes 41287680 | tf_op jit(solution)/shard_map/convert_element_type | solution.py:432
  1357.6 26.4 %maximum_convert_fusion = f32[768,17920]{1,0:T(8,128)} fusion(bf16[768,768]{1,0:T(8,128)(2,1)S(1)} %copy-done.28, bf16[768,8192]{1,0:T(8,128)(2,1)} %reshape.648, bf16[768,768]{1,0:T(8,128)(2,1)S(1)} %copy.204, bf16[768,8192]{1,0:T(8,128)(2,1)} %reshape.646), kind=kLoop, calls=%fused_computation.1 | loop fusion | flops 110100480 | bytes 82575360 | tf_op jit(solution)/shard_map/convert_element_type | solution.py:441
  (466 shorter events, 449.7 us)
Async XLA Ops:
  7.2 286.3 %all-gather.8.cloned.1.call-start = ((), (), s32[]{:S(2)}) async-start(), calls=%async_computation.5 | async-start | bytes 13369344 | tf_op jit(solution)/shard_map/all_gather | solution.py:193
  8.0 319.0 %all-gather.6.cloned.1.call-start = ((), (), s32[]{:S(2)}) async-start(), calls=%async_computation.3 | async-start | bytes 13369344 | tf_op jit(solution)/shard_map/all_gather | solution.py:264
  9.5 30.5 %collective-permute-start.2 = (bf16[1,2560]{1,0:T(2,128)(2,1)}, bf16[1,2560]{1,0:T(2,128)(2,1)}, u32[]{:S(2)}, u32[]{:S(2)}) collective-permute-start(bf16[1,2560]{1,0:T(2,128)(2,1)} %broadcast_in_dim.18), channel_id=1, source_target_pairs={{0,16},{16,0},{1,17},{17,1},{2,18},{18,2},{3,19},{19,3},{4,20},{20... | collective-permute-start | bytes 15368 | tf_op jit(solution)/shard_map/ppermute | solution.py:67
  15.9 33.4 %collective-permute-start.3 = (bf16[768,640]{1,0:T(8,128)(2,1)}, bf16[768,640]{1,0:T(8,128)(2,1)}, u32[]{:S(2)}, u32[]{:S(2)}) collective-permute-start(bf16[768,640]{1,0:T(8,128)(2,1)} %pad_maximum_fusion.26), channel_id=1, source_target_pairs={{0,16},{16,0},{1,17},{17,1},{2,18},{18,2},{3,19},{19,3},{4,20},{20... | collective-permute-start | bytes 2949128 | tf_op jit(solution)/shard_map/ppermute | solution.py:67
  15.9 19.9 %collective-permute-start = (bf16[2,2,64,1536]{3,2,1,0:T(8,128)(2,1)S(1)}, bf16[2,2,64,1536]{3,2,1,0:T(8,128)(2,1)}, u32[]{:S(2)}, u32[]{:S(2)}) collective-permute-start(bf16[2,2,64,1536]{3,2,1,0:T(8,128)(2,1)S(1)} %copy-done.6), channel_id=1, source_target_pairs={{0,2},{2,0},{1,3},{3,1},{4,6},{6,4},{5,7},{7,5},{8,10},{10,8},{9,1... | collective-permute-start | bytes 2359304 | tf_op jit(solution)/shard_map/ppermute | solution.py:67
  17.9 17.2 %collective-permute-start.4 = (s32[2,2,64]{2,1,0:T(2,128)S(1)}, s32[2,2,64]{2,1,0:T(2,128)}, u32[]{:S(2)}, u32[]{:S(2)}) collective-permute-start(s32[2,2,64]{2,1,0:T(2,128)S(1)} %copy-done.88), channel_id=1, source_target_pairs={{0,2},{2,0},{1,3},{3,1},{4,6},{6,4},{5,7},{7,5},{8,10},{10,8},{9,1... | collective-permute-start | bytes 3080 | tf_op jit(solution)/shard_map/ppermute | solution.py:67
  19.1 91.3 %collective-permute-start.12 = (bf16[384,1536]{1,0:T(8,128)(2,1)}, bf16[384,1536]{1,0:T(8,128)(2,1)}, u32[]{:S(2)}, u32[]{:S(2)}) collective-permute-start(bf16[384,1536]{1,0:T(8,128)(2,1)} %constant_dynamic-slice_fusion.12), channel_id=1, source_target_pairs={{0,16},{16,0},{1,17},{17,1},{2,18},{18,2},{3,19},{19,3},{4,20},{20... | collective-permute-start | bytes 3538952 | tf_op jit(solution)/shard_map/ppermute | solution.py:67
  65.1 16.6 %collective-permute-start.8 = (bf16[1024,128]{0,1:T(8,128)(2,1)S(1)}, bf16[1024,128]{0,1:T(8,128)(2,1)S(1)}, u32[]{:S(2)}, u32[]{:S(2)}) collective-permute-start(bf16[1024,128]{0,1:T(8,128)(2,1)S(1)} %get-tuple-element.16), channel_id=1, source_target_pairs={{12,0},{0,4},{4,8},{8,12},{13,1},{1,5},{5,9},{9,13},{14,2},{2,6},{... | collective-permute-start | bytes 786440 | tf_op jit(solution)/shard_map/ppermute | solution.py:72
  66.7 31.7 %collective-permute-start.7 = (bf16[1024,128]{0,1:T(8,128)(2,1)S(1)}, bf16[1024,128]{0,1:T(8,128)(2,1)S(1)}, u32[]{:S(2)}, u32[]{:S(2)}) collective-permute-start(bf16[1024,128]{0,1:T(8,128)(2,1)S(1)} %get-tuple-element.16), channel_id=1, source_target_pairs={{8,0},{12,4},{0,8},{4,12},{9,1},{13,5},{1,9},{5,13},{10,2},{14,6},... | collective-permute-start | bytes 786440 | tf_op jit(solution)/shard_map/ppermute | solution.py:72
  69.2 30.9 %collective-permute-start.6 = (bf16[1024,128]{0,1:T(8,128)(2,1)S(1)}, bf16[1024,128]{0,1:T(8,128)(2,1)S(1)}, u32[]{:S(2)}, u32[]{:S(2)}) collective-permute-start(bf16[1024,128]{0,1:T(8,128)(2,1)S(1)} %get-tuple-element.16), channel_id=1, source_target_pairs={{4,0},{8,4},{12,8},{0,12},{5,1},{9,5},{13,9},{1,13},{6,2},{10,6},{... | collective-permute-start | bytes 786440 | tf_op jit(solution)/shard_map/ppermute | solution.py:72
  101.1 20.8 %collective-permute-start.9 = (bf16[3,1024,128]{1,2,0:T(8,128)(2,1)}, bf16[3,1024,128]{1,2,0:T(8,128)(2,1)}, u32[]{:S(2)}, u32[]{:S(2)}) collective-permute-start(bf16[3,1024,128]{1,2,0:T(8,128)(2,1)} %pad_maximum_fusion.27), channel_id=1, source_target_pairs={{0,1},{1,0},{2,3},{3,2},{4,5},{5,4},{6,7},{7,6},{8,9},{9,8},{10,11... | collective-permute-start | bytes 2359304 | tf_op jit(solution)/shard_map/ppermute | solution.py:67
  110.4 47.2 %collective-permute-start.13 = (bf16[384,1536]{1,0:T(8,128)(2,1)}, bf16[384,1536]{1,0:T(8,128)(2,1)}, u32[]{:S(2)}, u32[]{:S(2)}) collective-permute-start(bf16[384,1536]{1,0:T(8,128)(2,1)} %collective-permute-done.12), channel_id=1, source_target_pairs={{0,1},{1,0},{2,3},{3,2},{4,5},{5,4},{6,7},{7,6},{8,9},{9,8},{10,11... | collective-permute-start | bytes 3538952 | tf_op jit(solution)/shard_map/ppermute | solution.py:67
  172.7 351.8 %reduce-scatter.8.cloned.1.call-start = ((), (), s32[]{:S(2)}) async-start(), calls=%async_computation.6 | async-start | bytes 13369344 | tf_op jit(solution)/shard_map/reduce_scatter | solution.py:290
  196.6 92.4 %collective-permute-start.14 = (bf16[768,1680]{0,1:T(8,128)(2,1)}, bf16[768,1680]{0,1:T(8,128)(2,1)}, u32[]{:S(2)}, u32[]{:S(2)}) collective-permute-start(bf16[768,1680]{0,1:T(8,128)(2,1)} %constant_dynamic-update-slice_fusion), channel_id=1, source_target_pairs={{0,16},{16,0},{1,17},{17,1},{2,18},{18,2},{3,19},{19,3},{4,20},{20... | collective-permute-start | bytes 7741448 | tf_op jit(solution)/shard_map/ppermute | solution.py:67
  389.3 352.8 %reduce-scatter.10.cloned.1.call-start = ((), (), s32[]{:S(2)}) async-start(), calls=%async_computation.9 | async-start | bytes 3096576 | tf_op jit(solution)/shard_map/reduce_scatter | solution.py:415
  527.5 18.6 %collective-permute-start.15 = (bf16[2,2,64,1536]{3,2,1,0:T(8,128)(2,1)S(1)}, bf16[2,2,64,1536]{3,2,1,0:T(8,128)(2,1)S(1)}, u32[]{:S(2)}, u32[]{:S(2)}) collective-permute-start(bf16[2,2,64,1536]{3,2,1,0:T(8,128)(2,1)S(1)} %bitcast.296), channel_id=1, source_target_pairs={{0,2},{2,0},{1,3},{3,1},{4,6},{6,4},{5,7},{7,5},{8,10},{10,8},{9,1... | collective-permute-start | bytes 2359304 | tf_op jit(solution)/shard_map/ppermute | solution.py:67
  598.8 20.5 %collective-permute-start.17 = (bf16[8,2,256,128]{2,3,0,1:T(8,128)(2,1)}, bf16[8,2,256,128]{2,3,0,1:T(8,128)(2,1)}, u32[]{:S(2)}, u32[]{:S(2)}) collective-permute-start(bf16[8,2,256,128]{2,3,0,1:T(8,128)(2,1)} %fusion.54), channel_id=1, source_target_pairs={{0,1},{1,0},{2,3},{3,2},{4,5},{5,4},{6,7},{7,6},{8,9},{9,8},{10,11... | collective-permute-start | bytes 3145736 | tf_op jit(solution)/shard_map/ppermute | solution.py:67
  628.5 18.6 %collective-permute-start.19 = (bf16[1024,128]{0,1:T(8,128)(2,1)}, bf16[1024,128]{0,1:T(8,128)(2,1)}, u32[]{:S(2)}, u32[]{:S(2)}) collective-permute-start(bf16[1024,128]{0,1:T(8,128)(2,1)} %convert_element_type.311), channel_id=1, source_target_pairs={{8,0},{12,4},{0,8},{4,12},{9,1},{13,5},{1,9},{5,13},{10,2},{14,6},... | collective-permute-start | bytes 786440 | tf_op jit(solution)/shard_map/ppermute | solution.py:72
  666.5 271.3 %reduce-scatter.6.cloned.1.call-start = ((), (), s32[]{:S(2)}) async-start(), calls=%async_computation.4 | async-start | bytes 13369344 | tf_op jit(solution)/shard_map/reduce_scatter | solution.py:313
  683.0 263.2 %all-gather.12.cloned.1.call-start = ((), (), s32[]{:S(2)}) async-start(), calls=%async_computation.8 | async-start | bytes 5849088 | tf_op jit(solution)/shard_map/all_gather | solution.py:418
  742.1 409.5 %all-gather.10.cloned.1.call-start = ((), (), s32[]{:S(2)}) async-start(), calls=%async_computation.7 | async-start | bytes 43868160 | tf_op jit(solution)/shard_map/all_gather | solution.py:310
  779.8 57.1 %collective-permute-start.28 = (bf16[2,384,1680]{1,2,0:T(8,128)(2,1)S(1)}, bf16[2,384,1680]{1,2,0:T(8,128)(2,1)}, u32[]{:S(2)}, u32[]{:S(2)}) collective-permute-start(bf16[2,384,1680]{1,2,0:T(8,128)(2,1)S(1)} %select_bitcast_fusion), channel_id=1, source_target_pairs={{0,2},{2,0},{1,3},{3,1},{4,6},{6,4},{5,7},{7,5},{8,10},{10,8},{9,1... | collective-permute-start | bytes 7741448 | tf_op jit(solution)/shard_map/ppermute | solution.py:67
  842.3 37.7 %collective-permute-start.29 = (bf16[384,1680]{0,1:T(8,128)(2,1)}, bf16[384,1680]{0,1:T(8,128)(2,1)}, u32[]{:S(2)}, u32[]{:S(2)}) collective-permute-start(bf16[384,1680]{0,1:T(8,128)(2,1)} %dynamic-slice_bitcast_fusion), channel_id=1, source_target_pairs={{0,16},{16,0},{1,17},{17,1},{2,18},{18,2},{3,19},{19,3},{4,20},{20... | collective-permute-start | bytes 3870728 | tf_op jit(solution)/shard_map/ppermute | solution.py:67
  895.4 21.7 %collective-permute-start.22 = (bf16[2,2,64,1536]{3,2,1,0:T(8,128)(2,1)}, bf16[2,2,64,1536]{3,2,1,0:T(8,128)(2,1)}, u32[]{:S(2)}, u32[]{:S(2)}) collective-permute-start(bf16[2,2,64,1536]{3,2,1,0:T(8,128)(2,1)} %fusion.60), channel_id=1, source_target_pairs={{0,2},{2,0},{1,3},{3,1},{4,6},{6,4},{5,7},{7,5},{8,10},{10,8},{9,1... | collective-permute-start | bytes 2359304 | tf_op jit(solution)/shard_map/ppermute | solution.py:67
  (106 other events, 2330.2 us)
Sparse Core Ops, SparseCore 0:
  10.4 127.0 all-gather.7
  172.9 154.0 all-gather.5
  389.4 135.0 reduce-scatter.7
  666.6 75.4 reduce-scatter.9
  746.6 138.3 reduce-scatter.5
  887.1 58.9 all-gather.11
  948.3 203.2 all-gather.9

commit v2 on v1

v2 whole, which is shorter than its diff:
```python
import jax
import jax.numpy as jnp
from jax import lax
from jax.sharding import Mesh, PartitionSpec as P

QUERY_HEADS = 12
KEY_VALUE_HEADS = 2
HEAD_SIZE = 128
LANES = 128

norm_eps = 1e-06
rope_theta = 1000000.0
masked_score = -1e30

WIDE = "wide"
PLANE = ("blk", "hx", "core")
f32, bf16 = jnp.float32, jnp.bfloat16


def rms_parts(values, gain_row):
    inverse = lax.rsqrt(jnp.mean(values * values, axis=-1, keepdims=True) + norm_eps)
    scaled = values * inverse
    return (scaled * gain_row, scaled, inverse)


def rms_back(grad_normed, scaled, inverse, gain_row):
    grad_scaled = grad_normed * gain_row
    mean_term = jnp.mean(grad_scaled * scaled, axis=-1, keepdims=True)
    return (inverse * (grad_scaled - scaled * mean_term), jnp.sum(grad_normed * scaled, axis=0))


def turn_back(values, cosine_table, sine_values):
    half_size = values.shape[-1] // 2
    turned = values * sine_values
    turned = jnp.concatenate([turned[..., half_size:], turned[..., :half_size]], axis=-1)
    return values * cosine_table + turned


def rope_tables(positions):
    frequency = rope_theta ** (-jnp.arange(0, HEAD_SIZE, 2).astype(f32) / HEAD_SIZE)
    angles = positions.astype(f32)[:, None] * frequency[None, :]
    cosine, sine = jnp.cos(angles), jnp.sin(angles)
    return (
        jnp.concatenate([cosine, cosine], axis=-1),
        jnp.concatenate([-sine, sine], axis=-1),
    )


def dot(a, b):
    return jnp.dot(a, b, preferred_element_type=f32)


def dot_rows(a, b):
    return lax.dot_general(a, b, (((0,), (0,)), ((), ())), preferred_element_type=f32)


def dot_cols(a, b):
    return lax.dot_general(a, b, (((1,), (1,)), ((), ())), preferred_element_type=f32)


def partner(values, axis, distance=1):
    count = lax.axis_size(axis)
    return lax.ppermute(values, axis, [(i, i ^ distance) for i in range(count)])


def shifted(values, axis, distance):
    count = lax.axis_size(axis)
    return lax.ppermute(values, axis, [((i + distance) % count, i) for i in range(count)])


def in_order(pieces, index):
    bit = 1
    while bit < len(pieces):
        odd = (index & bit) != 0
        pieces = [jnp.where(odd, pieces[k ^ bit], pieces[k]) for k in range(len(pieces))]
        bit *= 2
    return pieces


def row_places(index, x_at, rows_dev):
    x_rel = (index // rows_dev) % 2
    core = index // (2 * rows_dev)
    x_abs = jnp.where(x_at == 0, x_rel, 1 - x_rel)
    return (2 * x_abs + core) * rows_dev + index % rows_dev


def on_device(
    tokens,
    positions,
    block_order,
    w_qkv,
    qkv_bias,
    w_out,
    w_gate_up,
    w_down,
    gain_attn,
    gain_mlp,
    cotangent,
):
    slot_count, seq_count, rows_dev, width = tokens.shape
    blk_count, x_count, core_count = (lax.axis_size(a) for a in ("blk", "hx", "core"))
    wide_count = lax.axis_size(WIDE)
    wide_at, blk_at, x_at, core_at = (lax.axis_index(a) for a in (WIDE, "blk", "hx", "core"))
    head_at = x_at * core_count + core_at
    head_shards = x_count * core_count
    heads_here = QUERY_HEADS // head_shards
    q_here = heads_here * HEAD_SIZE
    q_total = QUERY_HEADS * HEAD_SIZE
    kv_total = KEY_VALUE_HEADS * HEAD_SIZE
    kv_at = head_at * KEY_VALUE_HEADS // head_shards
    rows_wide = w_qkv.shape[0]
    half = rows_wide // 2
    block_rows = rows_dev * head_shards
    dev_rows = slot_count * seq_count * rows_dev
    blk_rows = dev_rows * head_shards
    ff = w_down.shape[1]
    others = range(1, wide_count)

    def by_wide(own, pieces):
        return jnp.concatenate(in_order([own] + pieces, wide_at), axis=0)

    def block_major(near, far):
        return jnp.moveaxis(jnp.stack(in_order([near, far], core_at)), (0, 1), (2, 3))

    def head_columns(array):
        return jnp.concatenate(
            [
                lax.dynamic_slice_in_dim(array, head_at * q_here, q_here, 1),
                lax.dynamic_slice_in_dim(array, q_total + kv_at * HEAD_SIZE, HEAD_SIZE, 1),
                lax.dynamic_slice_in_dim(
                    array, q_total + kv_total + kv_at * HEAD_SIZE, HEAD_SIZE, 1
                ),
            ],
            axis=1,
        )

    share = blk_count * x_count * core_count
    main = ff // (LANES * share) * LANES
    extra = (ff - share * main) // LANES
    ff_here = main + LANES

    def ff_columns():
        at = blk_at * x_count + x_at
        has = (core_at == 0) & (at < extra)
        columns = []
        for array, first in ((w_down, 0), (w_gate_up, 0), (w_gate_up, ff)):
            more = lax.dynamic_slice_in_dim(array, first + share * main + at * LANES, LANES, 1)
            columns += [
                lax.dynamic_slice_in_dim(
                    array, first + (at * core_count + core_at) * main, main, 1
                ),
                jnp.where(has, more, jnp.zeros_like(more)),
            ]
        return jnp.concatenate(columns, axis=1)

    tokens_x = partner(tokens, "hx")
    positions_x = partner(positions, "hx")
    small = jnp.concatenate([qkv_bias, gain_attn, gain_mlp])[None]
    small = by_wide(small, [partner(small, WIDE, d) for d in others])
    w_head_own = head_columns(w_qkv)
    w_head_far = [partner(w_head_own, WIDE, d) for d in others]
    cot_rows = cotangent.reshape(-1, width)
    group_cotangent = lax.all_gather(cot_rows, PLANE, axis=0, tiled=True)
    w_out_half = lax.dynamic_slice_in_dim(w_out, core_at * half, half, 0)
    w_out_far = [partner(w_out_half, WIDE, d) for d in others]
    bias_len = qkv_bias.shape[0]
    bias_row = small[:, :bias_len].reshape(1, -1).astype(f32)
    gain_attn_row = small[:, bias_len : bias_len + rows_wide].reshape(1, -1).astype(f32)
    gain_mlp_row = small[:, bias_len + rows_wide :].reshape(1, -1).astype(f32)

    tokens_pair = jnp.stack([tokens, tokens_x])
    positions_pair = jnp.stack([positions, positions_x])
    blk_tokens = block_major(tokens_pair, partner(tokens_pair, "core")).reshape(-1, width)
    blk_positions = block_major(positions_pair, partner(positions_pair, "core")).reshape(-1)
    cosine_table, sine_values = rope_tables(blk_positions)
    w_head = by_wide(w_head_own, w_head_far)
    normed_attn = rms_parts(blk_tokens.astype(f32), gain_attn_row)[0].astype(bf16)
    projected = dot(normed_attn, w_head) + head_columns(bias_row)

    def turned(values):
        moved = jnp.concatenate(
            [values[..., HEAD_SIZE // 2 :], values[..., : HEAD_SIZE // 2]], axis=-1
        )
        return (values * cosine_table[:, None] + moved * sine_values[:, None]).astype(bf16)

    queries = turned(projected[:, :q_here].reshape(-1, heads_here, HEAD_SIZE)).reshape(-1, q_here)
    own_keys = turned(projected[:, None, q_here : q_here + HEAD_SIZE])[:, 0]
    own_values = projected[:, q_here + HEAD_SIZE :].astype(bf16)
    pair = [own_keys, own_values]
    sent = jnp.where(core_at == 0, pair[0], pair[1])
    ff_own = ff_columns()
    ff_far = [partner(ff_own, WIDE, d) for d in others]
    arrived = [shifted(sent, "blk", d) for d in range(1, blk_count)]
    arrived = jnp.stack(arrived)
    other = partner(arrived, "core")
    kv_shape = (blk_count * slot_count, seq_count, block_rows, HEAD_SIZE)
    all_keys, all_values = (
        jnp.concatenate([own[None], far]).reshape(kv_shape)
        for own, far in zip(pair, in_order([arrived, other], core_at))
    )
    key_slots = (
        (blk_at + jnp.arange(blk_count, dtype=jnp.int32)) % blk_count * slot_count
    )[:, None] + jnp.arange(slot_count, dtype=jnp.int32)[None]
    key_order = jnp.take(block_order, key_slots.reshape(-1))

    query_order = key_order[:slot_count]
    places = row_places(jnp.arange(block_rows, dtype=jnp.int32), x_at, rows_dev)
    queries = queries.reshape(slot_count, seq_count, block_rows, heads_here, HEAD_SIZE)
    scale = HEAD_SIZE**-0.5
    allowed = (
        places[None, None, None, None, None, :]
        <= places[None, None, :, None, None, None]
        + (query_order[:, None] - key_order[None, :])[:, None, None, None, :, None] * block_rows
    )
    scores = jnp.einsum("asrhd,kscd->asrhkc", queries, all_keys, preferred_element_type=f32)
    masked = jnp.where(allowed, scores * scale, masked_score)
    peak = jnp.max(masked, axis=(-2, -1), keepdims=True)
    weights = jnp.exp(masked - peak)
    total = jnp.sum(weights, axis=(-2, -1), keepdims=True)
    log_total = peak + jnp.log(total)
    attention = jnp.einsum(
        "asrhkc,kscd->asrhd", (weights / total).astype(bf16), all_values, preferred_element_type=f32
    )
    attended_head = attention.astype(bf16).reshape(blk_rows, q_here)
    back = attended_head.reshape(slot_count, seq_count, 2, 2, rows_dev, q_here)
    back_x = back[:, :, :, 1]
    from_x = partner(back_x, "hx")

    out_far = [
        jnp.concatenate(in_order([far, partner(far, "core")], core_at), axis=0)
        for far in w_out_far
    ]
    full_out = by_wide(w_out, out_far)
    w_out_head = lax.dynamic_slice_in_dim(full_out, head_at * q_here, q_here, 1)
    w_ff = by_wide(ff_own, ff_far)

    by_x = jnp.stack([back[:, :, :, 0], from_x])
    own_c, other_c = in_order([by_x[:, :, :, 0], by_x[:, :, :, 1]], core_at)
    by_core = in_order([own_c, partner(other_c, "core")], core_at)
    by_head = [
        piece for x_piece in zip(*(in_order(list(p), x_at) for p in by_core)) for piece in x_piece
    ]
    attended = jnp.concatenate(by_head, axis=-1).reshape(dev_rows, q_total)
    flat_tokens = tokens.reshape(-1, width).astype(f32)
    middle = flat_tokens + dot_cols(attended, full_out)
    normed_mlp = rms_parts(middle, gain_mlp_row)[0].astype(bf16)

    normed_mlp, group_cotangent = lax.optimization_barrier((normed_mlp, group_cotangent))
    group_normed = lax.all_gather(normed_mlp, PLANE, axis=0, tiled=True)
    w_down_here, w_gate_up_here = w_ff[:, :ff_here], w_ff[:, ff_here:]
    grad_hidden = dot(group_cotangent, w_down_here)
    gate_up = dot(group_normed, w_gate_up_here)
    gate, up = gate_up[:, :ff_here], gate_up[:, ff_here:]
    sigmoid = jax.nn.sigmoid(gate)
    silu = gate * sigmoid
    hidden = (silu * up).astype(bf16)
    grad_gate = (grad_hidden * up * (sigmoid + silu * (1.0 - sigmoid))).astype(bf16)
    grad_up = (grad_hidden * silu).astype(bf16)
    grad_gate_up = jnp.concatenate([grad_gate, grad_up], axis=1)
    grad_part = dot_cols(grad_gate_up, w_gate_up_here).astype(bf16)
    grad_normed_mlp = lax.psum_scatter(grad_part, PLANE, scatter_dimension=0, tiled=True)
    down_part = dot_rows(group_cotangent, hidden).astype(bf16)
    gate_part = dot_rows(group_normed, grad_gate).astype(bf16)
    up_part = dot_rows(group_normed, grad_up).astype(bf16)

    def over_wide(part):
        parts = part.reshape(wide_count, rows_wide, -1)
        total = lax.dynamic_index_in_dim(parts, wide_at, 0, keepdims=False).astype(f32)
        for d in others:
            theirs = lax.dynamic_index_in_dim(parts, wide_at ^ d, 0, keepdims=False)
            total = total + partner(theirs, WIDE, d).astype(f32)
        return total.astype(bf16)

    sums_ff = [over_wide(part) for part in (down_part, gate_part, up_part)]
    grad_normed_mlp, *sums_ff = lax.optimization_barrier((grad_normed_mlp, *sums_ff))
    ff_all = lax.all_gather(
        jnp.concatenate(
            [total[:, :main] for total in sums_ff] + [total[:, main:] for total in sums_ff],
            axis=1,
        ),
        PLANE,
        axis=0,
    )

    _, scaled_mlp, inverse_mlp = rms_parts(middle, gain_mlp_row)
    grad_middle, grad_gain_mlp = rms_back(
        grad_normed_mlp.astype(f32), scaled_mlp, inverse_mlp, gain_mlp_row
    )
    grad_middle = cotangent.reshape(-1, width).astype(f32) + grad_middle
    grad_branch = grad_middle.astype(bf16).reshape(tokens.shape)
    branch_pair = jnp.stack([grad_branch, partner(grad_branch, "hx")])

    blk_branch = block_major(branch_pair, partner(branch_pair, "core")).reshape(-1, width)
    grad_heads = dot(blk_branch, w_out_head).astype(bf16)
    hidden, grad_heads = lax.optimization_barrier((hidden, grad_heads))
    out_part = dot_cols(hidden, w_down_here).astype(bf16)
    grad_heads = grad_heads.reshape(queries.shape)
    row_inner = jnp.sum(grad_heads.astype(f32) * attention, axis=-1)
    probs = jnp.exp(masked - log_total)
    grad_probs = jnp.einsum(
        "asrhd,kscd->asrhkc", grad_heads, all_values, preferred_element_type=f32
    )
    grad_scores = (probs * (grad_probs - row_inner[..., None, None])).astype(bf16)
    grad_queries = (
        jnp.einsum("asrhkc,kscd->asrhd", grad_scores, all_keys, preferred_element_type=f32) * scale
    )
    grad_queries = turn_back(
        grad_queries.reshape(-1, heads_here, HEAD_SIZE),
        cosine_table[:, None, :],
        sine_values[:, None, :],
    ).reshape(-1, q_here)
    grad_keys = (
        jnp.einsum("asrhkc,asrhd->kscd", grad_scores, queries, preferred_element_type=f32) * scale
    )
    grad_values = jnp.einsum(
        "asrhkc,asrhd->kscd", probs.astype(bf16), grad_heads, preferred_element_type=f32
    )
    kept, given = in_order([grad_keys, grad_values], core_at)
    kept = kept + partner(given.astype(bf16), "core").astype(f32)
    kept = kept.reshape(blk_count, blk_rows, HEAD_SIZE)
    sent_pair = [kept[blk_count - d].astype(bf16) for d in range(1, blk_count)]
    out_grad_part = dot_rows(blk_branch, attended_head)
    grad_pair = kept[0]
    for d in range(1, blk_count):
        grad_pair = grad_pair + shifted(sent_pair[d - 1], "blk", d).astype(f32)
    grad_pair = jnp.where(
        core_at == 0, turn_back(grad_pair, cosine_table, sine_values), grad_pair
    )
    grad_projected = jnp.concatenate([grad_queries, grad_pair], axis=1).astype(bf16)
    w_back = jnp.concatenate(
        [
            w_head[:, :q_here],
            jnp.where(
                core_at == 0,
                w_head[:, q_here : q_here + HEAD_SIZE],
                w_head[:, q_here + HEAD_SIZE :],
            ),
        ],
        axis=1,
    )
    back_part = dot_cols(grad_projected, w_back).astype(bf16)
    back_part = back_part.reshape(slot_count, seq_count, 2, 2, rows_dev, width)
    own_c, other_c = in_order([back_part[:, :, 0], back_part[:, :, 1]], core_at)

    qkv_part = dot_rows(normed_attn, grad_projected)
    proj_part = jnp.concatenate(
        [qkv_part[:, :q_here], out_grad_part, qkv_part[:, q_here:]], axis=1
    ).astype(bf16)
    proj_part = proj_part.reshape(wide_count, rows_wide, -1)
    proj_sum = lax.dynamic_index_in_dim(proj_part, wide_at, 0, keepdims=False).astype(f32)
    for d in others:
        theirs = lax.dynamic_index_in_dim(proj_part, wide_at ^ d, 0, keepdims=False)
        proj_sum = proj_sum + partner(theirs, WIDE, d).astype(f32)

    own_c = own_c.astype(f32) + partner(other_c, "core").astype(f32)
    given_x = own_c[:, :, 1].astype(bf16)
    grad_normed_attn = own_c[:, :, 0] + partner(given_x, "hx").astype(f32)
    proj_parts = proj_sum.reshape(blk_count, rows_wide // blk_count, -1)
    proj_done = lax.dynamic_index_in_dim(proj_parts, blk_at, 0, keepdims=False)
    for d in range(1, blk_count):
        theirs = lax.dynamic_index_in_dim(proj_parts, blk_at ^ d, 0, keepdims=False)
        proj_done = proj_done + partner(theirs.astype(bf16), "blk", d).astype(f32)
    grad_normed_attn = grad_normed_attn.reshape(-1, width)
    scaled_attn, inverse_attn = rms_parts(flat_tokens, gain_attn_row)[1:]
    grad_flat, grad_gain_attn = rms_back(
        grad_normed_attn, scaled_attn, inverse_attn, gain_attn_row
    )
    input_grad = (grad_middle + grad_flat).astype(bf16).reshape(tokens.shape)
    proj_done = proj_done.astype(bf16)
    proj_blk = [proj_done] + [partner(proj_done, "blk", d) for d in range(1, blk_count)]
    proj_rows = jnp.concatenate(in_order(proj_blk, blk_at))
    proj_rows, ff_all = lax.optimization_barrier((proj_rows, ff_all))
    proj_pair = jnp.stack(in_order([proj_rows, partner(proj_rows, "hx")], x_at))
    proj_all = in_order([proj_pair, partner(proj_pair, "core")], core_at)

    column_sums = jnp.sum(grad_projected.astype(f32), axis=0)
    bias_sum = jnp.zeros((q_total + 2 * kv_total,), f32)
    bias_sum = lax.dynamic_update_slice(bias_sum, column_sums[:q_here], (head_at * q_here,))
    bias_sum = lax.dynamic_update_slice(
        bias_sum,
        column_sums[q_here:],
        (q_total + core_at * kv_total + kv_at * HEAD_SIZE,),
    )
    sums = jnp.concatenate([bias_sum, grad_gain_attn, grad_gain_mlp.reshape(-1)]).reshape(-1, LANES)
    for axis in ("core", "hx", "blk", WIDE):
        step = 1
        while step < lax.axis_size(axis):
            sums = sums + partner(sums, axis, step)
            step *= 2
    sums = sums.reshape(-1)
    bias_at = q_total + 2 * kv_total
    bias_grad = lax.dynamic_slice_in_dim(sums, wide_at * bias_len, bias_len)
    gain_attn_grad = lax.dynamic_slice_in_dim(sums, bias_at + wide_at * rows_wide, rows_wide)
    gain_mlp_grad = lax.dynamic_slice_in_dim(
        sums, bias_at + width + wide_at * rows_wide, rows_wide
    )

    heads = [(x, c) for x in range(x_count) for c in range(core_count)]
    qkv_grad = jnp.concatenate(
        [proj_all[c][x, :, :q_here] for x, c in heads]
        + [proj_all[c][x, :, 2 * q_here :] for c in range(core_count) for x in range(x_count)],
        axis=1,
    ).astype(f32)
    out_grad = jnp.concatenate(
        [proj_all[c][x, :, q_here : 2 * q_here] for x, c in heads], axis=1
    ).astype(f32)

    def assembled(kinds):
        into = jnp.zeros((rows_wide, len(kinds) * ff), f32)
        at = 0
        for kind in kinds:
            pieces = [ff_all[p, :, kind * main : (kind + 1) * main] for p in range(share)]
            first = 3 * main + kind * LANES
            pieces += [ff_all[e * core_count, :, first : first + LANES] for e in range(extra)]
            for piece in pieces:
                into = lax.dynamic_update_slice(into, piece.astype(f32), (0, at))
                at += piece.shape[1]
        return into

    ff_all, out_part = lax.optimization_barrier((ff_all, out_part))
    down_grad, gate_up_grad = assembled([0]), assembled([1, 2])
    mlp_out = lax.psum_scatter(out_part, PLANE, scatter_dimension=0, tiled=True)
    output = (middle + mlp_out.astype(f32)).astype(bf16).reshape(tokens.shape)
    return (
        output,
        input_grad,
        qkv_grad,
        bias_grad,
        out_grad,
        gate_up_grad,
        down_grad,
        gain_attn_grad,
        gain_mlp_grad,
    )


def solution(mesh):
    wide, blk, head = mesh.devices.shape
    cores = 2
    fine = Mesh(
        mesh.devices.reshape(wide, blk, head // cores, cores), (WIDE, "blk", "hx", "core")
    )
    rows = P("blk", WIDE, ("hx", "core"), None)
    matrix, vector = P(WIDE, None), P(WIDE)
    in_specs = (
        rows,
        P("blk", WIDE, ("hx", "core")),
        P(),
        matrix,
        vector,
        matrix,
        matrix,
        matrix,
        vector,
        vector,
        rows,
    )
    out_specs = (rows, rows, matrix, vector, matrix, matrix, matrix, vector, vector)
    return jax.shard_map(
        on_device, mesh=fine, in_specs=in_specs, out_specs=out_specs, check_vma=False
    )
```

time: 1400 us -> 995 us (0.71)
  waiting for transfers between devices: 667 us -> 366 us
  local copies, waits for them, and re-layouts: 321 us -> 88.3 us
  other arithmetic: 164 us -> 251 us
  matrix products: 187 us -> 208 us
  starting transfers between devices: 36.2 us -> 57.1 us
    all_gather x4 -> x3, waiting for transfers between devices: 197 us -> 44.7 us  [the longest x1 44.7 us: on_device(): group_normed = lax.all_gather(normed_mlp, PLANE, axis=0, tiled=True)]
    dynamic_update_slice x0 -> x45, other arithmetic: none -> 150 us  [assembled(): into = lax.dynamic_update_slice(into, piece.astype(f32), (0, at))]
    reduce_scatter x3 -> x2, waiting for transfers between devices: 181 us -> 50 us  [the longest x1 50 us: on_device(): lax.psum_scatter(grad_part, PLANE, scatter_dimension=0, tiled=True)]
    transpose x8 -> x1, local copies, waits for them, and re-layouts: 123 us -> 0.27 us  [block_major(): jnp.moveaxis(jnp.stack(in_order([near, far], core_at)), (0, 1), (2, 3))]
    reshape x9 -> x1, local copies, waits for them, and re-layouts: 70 us -> 0.57 us  [on_device(): grad_heads = grad_heads.reshape(queries.shape)]
    convert_element_type x10 -> x9, other arithmetic: 77 us -> 17.8 us  [the longest x3 5.45 us: over_wide(): return total.astype(bf16)]
    ppermute x24 -> x34, waiting for transfers between devices: 255 us -> 230 us  [partner(): return lax.ppermute(values, axis, [(i, i ^ distance) for i in range(count)])]
    ppermute x24 -> x34, starting transfers between devices: 23.8 us -> 47.5 us  [partner(): return lax.ppermute(values, axis, [(i, i ^ distance) for i in range(count)])]
  transfers between devices with their start and end apart: 37 -> 45, of which waited for: 24 -> 23; matrix products, arithmetic and copies ran while one was open for 21% -> 46% of each run, Pallas kernels for 0% -> 0%
where the time goes in v2:
time: 995 us; the launch traced here: 985 us
  waiting for transfers between devices  366 us (37%)
  other arithmetic  251 us (25%)
  matrix products  208 us (21%)
  local copies, waits for them, and re-layouts  88.3 us (9%)
  starting transfers between devices  57.1 us (6%)
  between operations  15.7 us (2%)
    ppermute x34, waiting for transfers between devices, partner(): return lax.ppermute(values, axis, [(i, i ^ distance) for i in range(count)])  230 us
    dynamic_update_slice x45, other arithmetic, assembled(): into = lax.dynamic_update_slice(into, piece.astype(f32), (0, at))  150 us
    dot_general x5, matrix products, dot_rows(): lax.dot_general(a, b, (((0,), (0,)), ((), ())), preferred_element_type=f32)  51.1 us
    reduce_scatter x1, waiting for transfers between devices, on_device(): lax.psum_scatter(grad_part, PLANE, scatter_dimension=0, tiled=True)  50 us
    dot_general x4, matrix products, dot(): return jnp.dot(a, b, preferred_element_type=f32)  49.7 us
    ppermute x34, starting transfers between devices, partner(): return lax.ppermute(values, axis, [(i, i ^ distance) for i in range(count)])  47.5 us
    all_gather x1, waiting for transfers between devices, on_device(): group_normed = lax.all_gather(normed_mlp, PLANE, axis=0, tiled=True)  44.7 us
    dot_general x4, matrix products, dot_cols(): lax.dot_general(a, b, (((1,), (1,)), ((), ())), preferred_element_type=f32)  44.3 us
  transfers between devices with their start and end apart: 45, of which 23 were waited for; matrix products, arithmetic and copies ran while one was open for 46% of the time, Pallas kernels for 0%

profile of v2, /device:TPU:0, one launch (start us, length us, event | category | flops | bytes accessed | tf_op | source)
XLA Modules:
  0.0 985.0 jit_solution(14051803231632253111)
XLA Ops:
  25.9 15.4 %collective-permute-done = bf16[2,2,64,1536]{3,2,1,0:T(8,128)(2,1)} collective-permute-done((bf16[2,2,64,1536]{3,2,1,0:T(8,128)(2,1)}, bf16[2,2,64,1536]{3,2,1,0:T(8,128)(2,1)}, u32[]{:S(2)}, u32[]{:S(2)}) %collective-permute-start) | collective-permute-done | bytes 786464 | tf_op jit(solution)/shard_map/ppermute | solution.py:63
  78.3 18.9 %collective-permute-done.7 = bf16[1024,128]{0,1:T(8,128)(2,1)S(1)} collective-permute-done((bf16[1024,128]{0,1:T(8,128)(2,1)S(1)}, bf16[1024,128]{0,1:T(8,128)(2,1)S(1)}, u32[]{:S(2)}, u32[]{:S(2)}) %collective-permute-start.7) | collective-permute-done | bytes 262176 | tf_op jit(solution)/shard_map/ppermute | solution.py:68
  130.9 13.7 %bitcast_convert_fusion = (bf16[2,2,256,3,128]{2,4,3,0,1:T(8,128)(2,1)S(1)}, f32[2,128,2,256,3,1]{3,1,5,4,2,0:T(8,128)}) fusion(bf16[8,2,256,128,1,1]{3,2,1,0,5,4:T(8,128)(2,1)} %bitcast.603, f32[2,8,256,2,256,3]{4,2,5,3,1,0:T(8,128)} %copy-done.2, f32[2,2,256,3]{2,3,0,1:T(4,128)S(1)} %fusion.2, f32[2,2,256,3]{2,3,0,1:T(4,128)S(1)} %get-tuple-element.164, ...), kind=kOutput, calls=%fused_computation.162 | convolution fusion | flops 1642463232 | bytes 29646848 | tf_op jit(solution)/shard_map/asrhkc,kscd->asrhd/dot_general | solution.py:221
  171.2 65.5 %collective-permute-done.14 = bf16[768,1920]{1,0:T(8,128)(2,1)S(1)} collective-permute-done((bf16[768,1920]{1,0:T(8,128)(2,1)S(1)}, bf16[768,1920]{1,0:T(8,128)(2,1)S(1)}, u32[]{:S(2)}, u32[]{:S(2)}) %collective-permute-start.14) | collective-permute-done | bytes 2949152 | tf_op jit(solution)/shard_map/ppermute | solution.py:63
  238.8 44.7 %all-gather.7.cloned.1.call-done = bf16[4096,1536]{1,0:T(8,128)(2,1)} async-done(((bf16[256,1536]{1,0:T(8,128)(2,1)}), bf16[4096,1536]{1,0:T(8,128)(2,1)}) %all-gather.7.cloned.1.call-update) | async-done | bytes 12582928 | tf_op jit(solution)/shard_map/all_gather | solution.py:249
  283.5 22.7 %fusion.124 = f32[4096,1280]{0,1:T(8,128)} fusion(bf16[4096,1536]{1,0:T(8,128)(2,1)} %all-gather.7.cloned.1.call-done, bf16[768,1920]{1,0:T(8,128)(2,1)} %get-tuple-element.90, bf16[768,1920]{1,0:T(8,128)(2,1)S(1)} %get-tuple-element.89), kind=kOutput, calls=%fused_computation.405 | convolution fusion | flops 16113991680 | bytes 39452672 | tf_op jit(solution)/shard_map/dot_general | solution.py:50
  306.2 23.0 %multiply_convert_fusion.1 = (bf16[4096,640]{0,1:T(8,128)(2,1)}, bf16[4096,640]{0,1:T(8,128)(2,1)}, bf16[4096,640]{0,1:T(8,128)(2,1)}) fusion(f32[4096,1280]{0,1:T(8,128)} %fusion.124, bf16[4096,1536]{1,0:T(8,128)(2,1)} %all-gather.5.cloned.1.call-done, bf16[768,1920]{1,0:T(8,128)(2,1)S(1)} %get-tuple-element.89, bf16[768,1920]{1,0:T(8,128)(2,1)} %get-tuple-element.90), kind=kOutput, calls=%fused_computation.25 | convolution fusion | flops 8093696000 | bytes 55181312 | tf_op jit(solution)/shard_map/dot_general | solution.py:50
  329.1 22.9 %convolution_convert_fusion.1 = bf16[4096,1536]{1,0:T(8,128)(2,1)} fusion(bf16[4096,640]{0,1:T(8,128)(2,1)} %get-tuple-element.87, bf16[4096,640]{0,1:T(8,128)(2,1)} %get-tuple-element.86, bf16[768,1920]{1,0:T(8,128)(2,1)} %get-tuple-element.90, bf16[768,1920]{1,0:T(8,128)(2,1)S(1)} %get-tuple-element.89), kind=kOutput, calls=%fused_computation.12 | convolution fusion | flops 16141254656 | bytes 28966912 | tf_op jit(solution)/shard_map/dot_general | solution.py:58
  352.1 15.2 %convolution_convert_fusion.5 = bf16[1536,640]{1,0:T(8,128)(2,1)S(1)} fusion(bf16[4096,1536]{1,0:T(8,128)(2,1)} %all-gather.5.cloned.1.call-done, bf16[4096,640]{0,1:T(8,128)(2,1)} %get-tuple-element.29), kind=kOutput, calls=%fused_computation.43 | convolution fusion | flops 8054046720 | bytes 19791872 | tf_op jit(solution)/shard_map/dot_general | solution.py:54
  368.9 17.0 %convolution_convert_fusion.3 = bf16[1536,640]{1,0:T(8,128)(2,1)S(1)} fusion(bf16[4096,1536]{1,0:T(8,128)(2,1)} %all-gather.7.cloned.1.call-done, bf16[4096,640]{0,1:T(8,128)(2,1)} %get-tuple-element.87), kind=kOutput, calls=%fused_computation.41 | convolution fusion | flops 8054046720 | bytes 19791872 | tf_op jit(solution)/shard_map/dot_general | solution.py:54
  387.8 12.5 %convolution_convert_fusion.4 = bf16[1536,640]{1,0:T(8,128)(2,1)S(1)} fusion(bf16[4096,1536]{1,0:T(8,128)(2,1)S(1)} %bitcast.623, bf16[4096,640]{0,1:T(8,128)(2,1)} %get-tuple-element.86), kind=kOutput, calls=%fused_computation.42 | convolution fusion | flops 8054046720 | bytes 19791872 | tf_op jit(solution)/shard_map/dot_general | solution.py:54
  415.7 18.0 %collective-permute-done.16 = bf16[768,640]{1,0:T(8,128)(2,1)} collective-permute-done((bf16[768,640]{1,0:T(8,128)(2,1)}, bf16[768,640]{1,0:T(8,128)(2,1)}, u32[]{:S(2)}, u32[]{:S(2)}) %collective-permute-start.16) | collective-permute-done | bytes 983072 | tf_op jit(solution)/shard_map/ppermute | solution.py:63
  435.2 50.0 %reduce-scatter.3.cloned.1.call-done = bf16[256,1536]{1,0:T(8,128)(2,1)} async-done(((bf16[4096,1536]{1,0:T(8,128)(2,1)}), bf16[256,1536]{1,0:T(8,128)(2,1)}) %reduce-scatter.3.cloned.1.call-update) | async-done | bytes 786448 | tf_op jit(solution)/shard_map/reduce_scatter | solution.py:261
  495.0 31.1 %collective-permute-done.18 = bf16[2,2,64,1536]{3,2,1,0:T(8,128)(2,1)S(1)} collective-permute-done((bf16[2,2,64,1536]{3,2,1,0:T(8,128)(2,1)S(1)}, bf16[2,2,64,1536]{3,2,1,0:T(8,128)(2,1)S(1)}, u32[]{:S(2)}, u32[]{:S(2)}) %collective-permute-start.18) | collective-permute-done | bytes 786464 | tf_op jit(solution)/shard_map/ppermute | solution.py:63
  540.2 15.9 %fusion.1 = bf16[2,2,256,3,8,256]{2,5,3,0,4,1:T(8,128)(2,1)} fusion(f32[2,8,256,2,256,3]{4,2,5,3,1,0:T(8,128)} %copy-done.2, f32[2,2,256,3]{2,3,0,1:T(4,128)S(1)} %fusion.46, f32[2,2,256,3]{2,3,0,1:T(4,128)S(1)} %log_add_fusion, pred[2,256,8,256]{1,3,0,2:T(8,128)(4,1)S(1)} %copy-done.27, bf16[8,2,256,128,1,1]{3,2,1,0,5,4:T(8,128)(2,1)} %bitcast.604, ...), kind=kOutput, calls=%fused_computation.4 | convolution fusion | flops 1648361472 | bytes 40656896 | tf_op jit(solution)/shard_map/asrhd,kscd->asrhkc/dot_general | solution.py:300
  565.2 12.1 %fusion.9 = f32[2,128,8,256,1,1]{3,1,5,4,2,0:T(8,128)S(1)} fusion(f32[2,8,256,2,256,3]{4,2,5,3,1,0:T(8,128)} %copy-done.2, f32[2,2,256,3]{2,3,0,1:T(4,128)S(1)} %log_add_fusion, pred[2,256,8,256]{1,3,0,2:T(8,128)(4,1)S(1)} %copy-done.27, bf16[2,2,256,3,128,1]{2,1,0,4,3,5:T(2,128)(2,1)S(1)} %bitcast.590), kind=kOutput, calls=%fused_computation.19 | convolution fusion | flops 1635778560 | bytes 29110272 | tf_op jit(solution)/shard_map/asrhkc,asrhd->kscd/dot_general | solution.py:315
  674.0 24.4 %collective-permute-done.24 = bf16[768,896]{0,1:T(8,128)(2,1)S(1)} collective-permute-done((bf16[768,896]{0,1:T(8,128)(2,1)S(1)}, bf16[768,896]{0,1:T(8,128)(2,1)S(1)}, u32[]{:S(2)}, u32[]{:S(2)}) %collective-permute-start.24) | collective-permute-done | bytes 1376288 | tf_op jit(solution)/shard_map/ppermute | solution.py:63
  713.7 10.5 %collective-permute-done.25 = bf16[192,896]{1,0:T(8,128)(2,1)S(1)} collective-permute-done((bf16[192,896]{1,0:T(8,128)(2,1)S(1)}, bf16[192,896]{1,0:T(8,128)(2,1)S(1)}, u32[]{:S(2)}, u32[]{:S(2)}) %collective-permute-start.25) | collective-permute-done | bytes 344096 | tf_op jit(solution)/shard_map/ppermute | solution.py:63
  724.2 16.4 %collective-permute-done.27 = bf16[192,896]{1,0:T(8,128)(2,1)S(1)} collective-permute-done((bf16[192,896]{1,0:T(8,128)(2,1)S(1)}, bf16[192,896]{1,0:T(8,128)(2,1)S(1)}, u32[]{:S(2)}, u32[]{:S(2)}) %collective-permute-start.27) | collective-permute-done | bytes 344096 | tf_op jit(solution)/shard_map/ppermute | solution.py:63
  740.6 14.9 %collective-permute-done.26 = bf16[192,896]{1,0:T(8,128)(2,1)S(1)} collective-permute-done((bf16[192,896]{1,0:T(8,128)(2,1)S(1)}, bf16[192,896]{1,0:T(8,128)(2,1)S(1)}, u32[]{:S(2)}, u32[]{:S(2)}) %collective-permute-start.26) | collective-permute-done | bytes 344096 | tf_op jit(solution)/shard_map/ppermute | solution.py:63
  764.3 18.1 %convolution_convert_fusion = bf16[4096,1536]{1,0:T(8,128)(2,1)} fusion(bf16[4096,640]{0,1:T(8,128)(2,1)} %get-tuple-element.29, bf16[768,1920]{1,0:T(8,128)(2,1)S(1)} %copy-done.42, bf16[768,1920]{1,0:T(8,128)(2,1)S(1)} %copy-done.43), kind=kOutput, calls=%fused_computation.11 | convolution fusion | flops 8063287296 | bytes 23724032 | tf_op jit(solution)/shard_map/dot_general | solution.py:58
  791.5 12.9 %collective-permute-start.38 = (f32[40,128]{1,0:T(8,128)S(1)}, f32[40,128]{1,0:T(8,128)S(1)}, u32[]{:S(2)}, u32[]{:S(2)}) collective-permute-start(f32[40,128]{1,0:T(8,128)S(1)} %add.508), channel_id=1, source_target_pairs={{0,8},{4,12},{8,0},{12,4},{1,9},{5,13},{9,1},{13,5},{2,10},{6,14},... | collective-permute-start | bytes 61448 | tf_op jit(solution)/shard_map/ppermute | solution.py:63
  814.2 23.5 %pad_convert_fusion = f32[768,17920]{1,0:T(8,128)} fusion(bf16[768,512]{1,0:T(8,128)(2,1)S(1)} %get-tuple-element.85), kind=kLoop, calls=%fused_computation.1 | loop fusion | flops 13762560 | bytes 55836672 | tf_op jit(solution)/shard_map/dynamic_update_slice | solution.py:416
  888.0 11.5 %pad_convert_fusion.1 = f32[768,8960]{1,0:T(8,128)} fusion(bf16[768,512]{1,0:T(8,128)(2,1)S(1)} %get-tuple-element.84), kind=kLoop, calls=%fused_computation.13 | loop fusion | flops 6881280 | bytes 28311552 | tf_op jit(solution)/shard_map/dynamic_update_slice | solution.py:416
  (511 shorter events, 438.5 us)
Async XLA Ops:
  7.2 156.5 %all-gather.5.cloned.1.call-start = ((), (), s32[]{:S(2)}) async-start(), calls=%async_computation.2 | async-start | bytes 13369344 | tf_op jit(solution)/shard_map/all_gather | solution.py:163
  7.9 275.6 %all-gather.7.cloned.1.call-start = ((), (), s32[]{:S(2)}) async-start(), calls=%async_computation.3 | async-start | bytes 13369344 | tf_op jit(solution)/shard_map/all_gather | solution.py:249
  12.3 33.3 %collective-permute-start.2 = (bf16[1,2560]{1,0:T(2,128)(2,1)}, bf16[1,2560]{1,0:T(2,128)(2,1)}, u32[]{:S(2)}, u32[]{:S(2)}) collective-permute-start(bf16[1,2560]{1,0:T(2,128)(2,1)} %broadcast_in_dim.18), channel_id=1, source_target_pairs={{0,16},{16,0},{1,17},{17,1},{2,18},{18,2},{3,19},{19,3},{4,20},{20... | collective-permute-start | bytes 15368 | tf_op jit(solution)/shard_map/ppermute | solution.py:63
  18.5 28.5 %collective-permute-start.3 = (bf16[768,640]{1,0:T(8,128)(2,1)}, bf16[768,640]{1,0:T(8,128)(2,1)}, u32[]{:S(2)}, u32[]{:S(2)}) collective-permute-start(bf16[768,640]{1,0:T(8,128)(2,1)} %pad_maximum_fusion.19), channel_id=1, source_target_pairs={{0,16},{16,0},{1,17},{17,1},{2,18},{18,2},{3,19},{19,3},{4,20},{20... | collective-permute-start | bytes 2949128 | tf_op jit(solution)/shard_map/ppermute | solution.py:63
  19.6 80.6 %collective-permute-start.12 = (bf16[384,1536]{1,0:T(8,128)(2,1)}, bf16[384,1536]{1,0:T(8,128)(2,1)}, u32[]{:S(2)}, u32[]{:S(2)}) collective-permute-start(bf16[384,1536]{1,0:T(8,128)(2,1)} %constant_dynamic-slice_fusion), channel_id=1, source_target_pairs={{0,16},{16,0},{1,17},{17,1},{2,18},{18,2},{3,19},{19,3},{4,20},{20... | collective-permute-start | bytes 3538952 | tf_op jit(solution)/shard_map/ppermute | solution.py:63
  63.3 34.0 %collective-permute-start.7 = (bf16[1024,128]{0,1:T(8,128)(2,1)S(1)}, bf16[1024,128]{0,1:T(8,128)(2,1)S(1)}, u32[]{:S(2)}, u32[]{:S(2)}) collective-permute-start(bf16[1024,128]{0,1:T(8,128)(2,1)S(1)} %get-tuple-element.40), channel_id=1, source_target_pairs={{8,0},{12,4},{0,8},{4,12},{9,1},{13,5},{1,9},{5,13},{10,2},{14,6},... | collective-permute-start | bytes 786440 | tf_op jit(solution)/shard_map/ppermute | solution.py:68
  65.8 32.0 %collective-permute-start.6 = (bf16[1024,128]{0,1:T(8,128)(2,1)S(1)}, bf16[1024,128]{0,1:T(8,128)(2,1)S(1)}, u32[]{:S(2)}, u32[]{:S(2)}) collective-permute-start(bf16[1024,128]{0,1:T(8,128)(2,1)S(1)} %get-tuple-element.40), channel_id=1, source_target_pairs={{4,0},{8,4},{12,8},{0,12},{5,1},{9,5},{13,9},{1,13},{6,2},{10,6},{... | collective-permute-start | bytes 786440 | tf_op jit(solution)/shard_map/ppermute | solution.py:68
  100.3 46.6 %collective-permute-start.13 = (bf16[384,1536]{1,0:T(8,128)(2,1)}, bf16[384,1536]{1,0:T(8,128)(2,1)}, u32[]{:S(2)}, u32[]{:S(2)}) collective-permute-start(bf16[384,1536]{1,0:T(8,128)(2,1)} %collective-permute-done.12), channel_id=1, source_target_pairs={{0,1},{1,0},{2,3},{3,2},{4,5},{5,4},{6,7},{7,6},{8,9},{9,8},{10,11... | collective-permute-start | bytes 3538952 | tf_op jit(solution)/shard_map/ppermute | solution.py:63
  163.7 321.4 %reduce-scatter.3.cloned.1.call-start = ((), (), s32[]{:S(2)}) async-start(), calls=%async_computation.4 | async-start | bytes 13369344 | tf_op jit(solution)/shard_map/reduce_scatter | solution.py:261
  170.4 66.4 %collective-permute-start.14 = (bf16[768,1920]{1,0:T(8,128)(2,1)S(1)}, bf16[768,1920]{1,0:T(8,128)(2,1)S(1)}, u32[]{:S(2)}, u32[]{:S(2)}) collective-permute-start(bf16[768,1920]{1,0:T(8,128)(2,1)S(1)} %select_dynamic-update-slice_fusion), channel_id=1, source_target_pairs={{0,16},{16,0},{1,17},{17,1},{2,18},{18,2},{3,19},{19,3},{4,20},{20... | collective-permute-start | bytes 8847368 | tf_op jit(solution)/shard_map/ppermute | solution.py:63
  352.1 459.2 %all-gather.9.cloned.1.call-start = ((), (), s32[]{:S(2)}) async-start(), calls=%async_computation.6 | async-start | bytes 50135040 | tf_op jit(solution)/shard_map/all_gather | solution.py:276
  367.5 36.5 %collective-permute-start.15 = (bf16[768,640]{1,0:T(8,128)(2,1)S(1)}, bf16[768,640]{1,0:T(8,128)(2,1)}, u32[]{:S(2)}, u32[]{:S(2)}) collective-permute-start(bf16[768,640]{1,0:T(8,128)(2,1)S(1)} %dynamic-slice_bitcast_fusion.3), channel_id=1, source_target_pairs={{0,16},{16,0},{1,17},{17,1},{2,18},{18,2},{3,19},{19,3},{4,20},{20... | collective-permute-start | bytes 2949128 | tf_op jit(solution)/shard_map/ppermute | solution.py:63
  402.6 31.1 %collective-permute-start.16 = (bf16[768,640]{1,0:T(8,128)(2,1)}, bf16[768,640]{1,0:T(8,128)(2,1)}, u32[]{:S(2)}, u32[]{:S(2)}) collective-permute-start(bf16[768,640]{1,0:T(8,128)(2,1)} %dynamic-slice_bitcast_fusion.2), channel_id=1, source_target_pairs={{0,16},{16,0},{1,17},{17,1},{2,18},{18,2},{3,19},{19,3},{4,20},{20... | collective-permute-start | bytes 2949128 | tf_op jit(solution)/shard_map/ppermute | solution.py:63
  492.2 482.1 %reduce-scatter.5.cloned.1.call-start = ((), (), s32[]{:S(2)}) async-start(), calls=%async_computation.5 | async-start | bytes 13369344 | tf_op jit(solution)/shard_map/reduce_scatter | solution.py:422
  493.5 32.6 %collective-permute-start.18 = (bf16[2,2,64,1536]{3,2,1,0:T(8,128)(2,1)S(1)}, bf16[2,2,64,1536]{3,2,1,0:T(8,128)(2,1)S(1)}, u32[]{:S(2)}, u32[]{:S(2)}) collective-permute-start(bf16[2,2,64,1536]{3,2,1,0:T(8,128)(2,1)S(1)} %bitcast.581), channel_id=1, source_target_pairs={{0,2},{2,0},{1,3},{3,1},{4,6},{6,4},{5,7},{7,5},{8,10},{10,8},{9,1... | collective-permute-start | bytes 2359304 | tf_op jit(solution)/shard_map/ppermute | solution.py:63
  592.3 33.8 %collective-permute-start.21 = (bf16[1024,128]{0,1:T(8,128)(2,1)}, bf16[1024,128]{0,1:T(8,128)(2,1)}, u32[]{:S(2)}, u32[]{:S(2)}) collective-permute-start(bf16[1024,128]{0,1:T(8,128)(2,1)} %convert_element_type.742), channel_id=1, source_target_pairs={{4,0},{8,4},{12,8},{0,12},{5,1},{9,5},{13,9},{1,13},{6,2},{10,6},{... | collective-permute-start | bytes 786440 | tf_op jit(solution)/shard_map/ppermute | solution.py:68
  665.5 32.8 %collective-permute-start.24 = (bf16[768,896]{0,1:T(8,128)(2,1)S(1)}, bf16[768,896]{0,1:T(8,128)(2,1)S(1)}, u32[]{:S(2)}, u32[]{:S(2)}) collective-permute-start(bf16[768,896]{0,1:T(8,128)(2,1)S(1)} %dynamic-slice_bitcast_fusion), channel_id=1, source_target_pairs={{0,16},{16,0},{1,17},{17,1},{2,18},{18,2},{3,19},{19,3},{4,20},{20... | collective-permute-start | bytes 4128776 | tf_op jit(solution)/shard_map/ppermute | solution.py:63
  670.7 39.5 %collective-permute-start.32 = (bf16[2,2,64,1536]{3,2,1,0:T(8,128)(2,1)S(1)}, bf16[2,2,64,1536]{3,2,1,0:T(8,128)(2,1)S(1)}, u32[]{:S(2)}, u32[]{:S(2)}) collective-permute-start(bf16[2,2,64,1536]{3,2,1,0:T(8,128)(2,1)S(1)} %fusion.59), channel_id=1, source_target_pairs={{0,2},{2,0},{1,3},{3,1},{4,6},{6,4},{5,7},{7,5},{8,10},{10,8},{9,1... | collective-permute-start | bytes 2359304 | tf_op jit(solution)/shard_map/ppermute | solution.py:63
  708.2 32.4 %collective-permute-start.27 = (bf16[192,896]{1,0:T(8,128)(2,1)S(1)}, bf16[192,896]{1,0:T(8,128)(2,1)S(1)}, u32[]{:S(2)}, u32[]{:S(2)}) collective-permute-start(bf16[192,896]{1,0:T(8,128)(2,1)S(1)} %get-tuple-element.110), channel_id=1, source_target_pairs={{0,12},{4,8},{8,4},{12,0},{1,13},{5,9},{9,5},{13,1},{2,14},{6,10},... | collective-permute-start | bytes 1032200 | tf_op jit(solution)/shard_map/ppermute | solution.py:63
  709.7 45.9 %collective-permute-start.26 = (bf16[192,896]{1,0:T(8,128)(2,1)S(1)}, bf16[192,896]{1,0:T(8,128)(2,1)S(1)}, u32[]{:S(2)}, u32[]{:S(2)}) collective-permute-start(bf16[192,896]{1,0:T(8,128)(2,1)S(1)} %get-tuple-element.111), channel_id=1, source_target_pairs={{0,8},{4,12},{8,0},{12,4},{1,9},{5,13},{9,1},{13,5},{2,10},{6,14},... | collective-permute-start | bytes 1032200 | tf_op jit(solution)/shard_map/ppermute | solution.py:63
  713.6 47.7 %collective-permute-start.35 = (f32[40,128]{1,0:T(8,128)S(1)}, f32[40,128]{1,0:T(8,128)S(1)}, u32[]{:S(2)}, u32[]{:S(2)}) collective-permute-start(f32[40,128]{1,0:T(8,128)S(1)} %maximum_bitcast_fusion.1), channel_id=1, source_target_pairs={{0,1},{1,0},{2,3},{3,2},{4,5},{5,4},{6,7},{7,6},{8,9},{9,8},{10,11... | collective-permute-start | bytes 61448 | tf_op jit(solution)/shard_map/ppermute | solution.py:63
  757.0 34.3 %collective-permute-start.29 = (bf16[192,896]{1,0:T(8,128)(2,1)S(1)}, bf16[192,896]{1,0:T(8,128)(2,1)S(1)}, u32[]{:S(2)}, u32[]{:S(2)}) collective-permute-start(bf16[192,896]{1,0:T(8,128)(2,1)S(1)} %fusion.75), channel_id=1, source_target_pairs={{0,8},{4,12},{8,0},{12,4},{1,9},{5,13},{9,1},{13,5},{2,10},{6,14},... | collective-permute-start | bytes 1032200 | tf_op jit(solution)/shard_map/ppermute | solution.py:63
  760.3 31.0 %collective-permute-start.28 = (bf16[192,896]{1,0:T(8,128)(2,1)S(1)}, bf16[192,896]{1,0:T(8,128)(2,1)S(1)}, u32[]{:S(2)}, u32[]{:S(2)}) collective-permute-start(bf16[192,896]{1,0:T(8,128)(2,1)S(1)} %fusion.75), channel_id=1, source_target_pairs={{0,12},{4,8},{8,4},{12,0},{1,13},{5,9},{9,5},{13,1},{2,14},{6,10},... | collective-permute-start | bytes 1032200 | tf_op jit(solution)/shard_map/ppermute | solution.py:63
  811.2 127.1 %collective-permute-start.33 = (bf16[768,896]{1,0:T(8,128)(2,1)S(1)}, bf16[768,896]{1,0:T(8,128)(2,1)}, u32[]{:S(2)}, u32[]{:S(2)}) collective-permute-start(bf16[768,896]{1,0:T(8,128)(2,1)S(1)} %pad_maximum_fusion.15), channel_id=1, source_target_pairs={{0,2},{2,0},{1,3},{3,1},{4,6},{6,4},{5,7},{7,5},{8,10},{10,8},{9,1... | collective-permute-start | bytes 4128776 | tf_op jit(solution)/shard_map/ppermute | solution.py:63
  (118 other events, 1485.6 us)
Sparse Core Ops, SparseCore 0:
  10.3 125.9 all-gather.4
  163.8 119.6 all-gather.6
  352.2 132.9 reduce-scatter.2
  492.3 273.5 all-gather.8
  812.9 134.2 reduce-scatter.4

commit v3 on v2

--- a/solution.py
+++ b/solution.py
@@ -249,6 +249,7 @@
     group_normed = lax.all_gather(normed_mlp, PLANE, axis=0, tiled=True)
     w_down_here, w_gate_up_here = w_ff[:, :ff_here], w_ff[:, ff_here:]
     grad_hidden = dot(group_cotangent, w_down_here)
+    grad_hidden, group_normed = lax.optimization_barrier((grad_hidden, group_normed))
     gate_up = dot(group_normed, w_gate_up_here)
     gate, up = gate_up[:, :ff_here], gate_up[:, ff_here:]
     sigmoid = jax.nn.sigmoid(gate)
@@ -366,10 +367,12 @@
         grad_normed_attn, scaled_attn, inverse_attn, gain_attn_row
     )
     input_grad = (grad_middle + grad_flat).astype(bf16).reshape(tokens.shape)
-    proj_done = proj_done.astype(bf16)
+    proj_done, ff_all, out_part = lax.optimization_barrier(
+        (proj_done.astype(bf16), ff_all, out_part)
+    )
+    mlp_out = lax.psum_scatter(out_part, PLANE, scatter_dimension=0, tiled=True)
     proj_blk = [proj_done] + [partner(proj_done, "blk", d) for d in range(1, blk_count)]
     proj_rows = jnp.concatenate(in_order(proj_blk, blk_at))
-    proj_rows, ff_all = lax.optimization_barrier((proj_rows, ff_all))
     proj_pair = jnp.stack(in_order([proj_rows, partner(proj_rows, "hx")], x_at))
     proj_all = in_order([proj_pair, partner(proj_pair, "core")], core_at)
 
@@ -417,9 +420,7 @@
                 at += piece.shape[1]
         return into
 
-    ff_all, out_part = lax.optimization_barrier((ff_all, out_part))
     down_grad, gate_up_grad = assembled([0]), assembled([1, 2])
-    mlp_out = lax.psum_scatter(out_part, PLANE, scatter_dimension=0, tiled=True)
     output = (middle + mlp_out.astype(f32)).astype(bf16).reshape(tokens.shape)
     return (
         output,

time: 995 us -> 973 us (0.978)
  waiting for transfers between devices: 366 us -> 350 us
  matrix products: 208 us -> 197 us
  other arithmetic: 251 us -> 261 us
    all_gather x1, waiting for transfers between devices: 44.7 us -> 28.2 us  [on_device(): group_normed = lax.all_gather(normed_mlp, PLANE, axis=0, tiled=True)]
    convert_element_type x1 -> x2, other arithmetic: 1.27 us -> 15.4 us  [the longest x1 14.1 us: on_device(): (grad_hidden * up * (sigmoid + silu * (1.0 - sigmoid))).astype(bf16)]
    unnamed x210 -> x214, local copies, waits for them, and re-layouts: 26.6 us -> 31 us
  transfers between devices with their start and end apart: 45 -> 45, of which waited for: 23 -> 21; matrix products, arithmetic and copies ran while one was open for 46% -> 48% of each run, Pallas kernels for 0% -> 0%
where the time goes in v3:
time: 973 us; the launch traced here: 964 us
  waiting for transfers between devices  350 us (36%)
  other arithmetic  261 us (27%)
  matrix products  197 us (20%)
  local copies, waits for them, and re-layouts  91.8 us (9%)
  starting transfers between devices  48.8 us (5%)
  between operations  15.7 us (2%)
    ppermute x34, waiting for transfers between devices, partner(): return lax.ppermute(values, axis, [(i, i ^ distance) for i in range(count)])  233 us
    dynamic_update_slice x45, other arithmetic, assembled(): into = lax.dynamic_update_slice(into, piece.astype(f32), (0, at))  150 us
    dot_general x5, matrix products, dot_rows(): lax.dot_general(a, b, (((0,), (0,)), ((), ())), preferred_element_type=f32)  49.2 us
    reduce_scatter x1, waiting for transfers between devices, on_device(): lax.psum_scatter(grad_part, PLANE, scatter_dimension=0, tiled=True)  48.9 us
    dot_general x4, matrix products, dot(): return jnp.dot(a, b, preferred_element_type=f32)  43.1 us
    dot_general x4, matrix products, dot_cols(): lax.dot_general(a, b, (((1,), (1,)), ((), ())), preferred_element_type=f32)  40.7 us
    ppermute x34, starting transfers between devices, partner(): return lax.ppermute(values, axis, [(i, i ^ distance) for i in range(count)])  39.3 us
    ppermute x6, waiting for transfers between devices, shifted(): lax.ppermute(values, axis, [((i + distance) % count, i) for i in range(co...  39.2 us
  transfers between devices with their start and end apart: 45, of which 21 were waited for; matrix products, arithmetic and copies ran while one was open for 48% of the time, Pallas kernels for 0%

profile of v3, /device:TPU:0, one launch (start us, length us, event | category | flops | bytes accessed | tf_op | source)
XLA Modules:
  0.0 963.8 jit_solution(6797263078523083059)
XLA Ops:
  25.9 15.4 %collective-permute-done = bf16[2,2,64,1536]{3,2,1,0:T(8,128)(2,1)} collective-permute-done((bf16[2,2,64,1536]{3,2,1,0:T(8,128)(2,1)}, bf16[2,2,64,1536]{3,2,1,0:T(8,128)(2,1)}, u32[]{:S(2)}, u32[]{:S(2)}) %collective-permute-start) | collective-permute-done | bytes 786464 | tf_op jit(solution)/shard_map/ppermute | solution.py:63
  78.3 18.9 %collective-permute-done.7 = bf16[1024,128]{0,1:T(8,128)(2,1)S(1)} collective-permute-done((bf16[1024,128]{0,1:T(8,128)(2,1)S(1)}, bf16[1024,128]{0,1:T(8,128)(2,1)S(1)}, u32[]{:S(2)}, u32[]{:S(2)}) %collective-permute-start.7) | collective-permute-done | bytes 262176 | tf_op jit(solution)/shard_map/ppermute | solution.py:68
  131.0 14.0 %bitcast_convert_fusion = (bf16[2,2,256,3,128]{2,4,3,0,1:T(8,128)(2,1)S(1)}, f32[2,128,2,256,3,1]{3,1,5,4,2,0:T(8,128)}) fusion(bf16[8,2,256,128,1,1]{3,2,1,0,5,4:T(8,128)(2,1)} %bitcast.605, f32[2,8,256,2,256,3]{4,2,5,3,1,0:T(8,128)} %copy-done.2, f32[2,2,256,3]{2,3,0,1:T(4,128)S(1)} %fusion.2, f32[2,2,256,3]{2,3,0,1:T(4,128)S(1)} %get-tuple-element.166, ...), kind=kOutput, calls=%fused_computation.160 | convolution fusion | flops 1642463232 | bytes 29646848 | tf_op jit(solution)/shard_map/asrhkc,kscd->asrhd/dot_general | solution.py:221
  170.5 65.7 %collective-permute-done.14 = bf16[768,1920]{1,0:T(8,128)(2,1)S(1)} collective-permute-done((bf16[768,1920]{1,0:T(8,128)(2,1)S(1)}, bf16[768,1920]{1,0:T(8,128)(2,1)S(1)}, u32[]{:S(2)}, u32[]{:S(2)}) %collective-permute-start.14) | collective-permute-done | bytes 2949152 | tf_op jit(solution)/shard_map/ppermute | solution.py:63
  239.2 15.6 %fusion.123 = f32[4096,640]{1,0:T(8,128)} fusion(bf16[4096,1536]{1,0:T(8,128)(2,1)} %all-gather.5.cloned.1.call-done, bf16[768,1920]{1,0:T(8,128)(2,1)S(1)} %get-tuple-element.92, bf16[768,1920]{1,0:T(8,128)(2,1)S(1)} %get-tuple-element.91), kind=kOutput, calls=%fused_computation.404 | convolution fusion | flops 8056995840 | bytes 28966912 | tf_op jit(solution)/shard_map/dot_general | solution.py:50
  254.8 28.2 %all-gather.7.cloned.1.call-done = bf16[4096,1536]{1,0:T(8,128)(2,1)} async-done(((bf16[256,1536]{1,0:T(8,128)(2,1)}), bf16[4096,1536]{1,0:T(8,128)(2,1)}) %all-gather.7.cloned.1.call-update) | async-done | bytes 12582928 | tf_op jit(solution)/shard_map/all_gather | solution.py:249
  283.0 23.4 %fusion.47 = f32[4096,1280]{1,0:T(8,128)} fusion(bf16[4096,1536]{1,0:T(8,128)(2,1)} %all-gather.7.cloned.1.call-done, bf16[768,1920]{1,0:T(8,128)(2,1)} %copy-done.41, bf16[768,1920]{1,0:T(8,128)(2,1)} %copy-done.40), kind=kOutput, calls=%fused_computation.175 | convolution fusion | flops 16113991680 | bytes 39452672 | tf_op jit(solution)/shard_map/dot_general | solution.py:50
  306.4 14.1 %multiply_convert_fusion.1 = (bf16[4096,640]{1,0:T(8,128)(2,1)S(1)}, bf16[4096,640]{1,0:T(8,128)(2,1)}, bf16[4096,640]{1,0:T(8,128)(2,1)}) fusion(f32[4096,640]{1,0:T(8,128)S(1)} %copy-done.13, f32[4096,1280]{1,0:T(8,128)} %fusion.47), kind=kLoop, calls=%fused_computation.25 | loop fusion | flops 36700160 | bytes 47185920 | tf_op jit(solution)/shard_map/convert_element_type | solution.py:258
  322.8 22.2 %convolution_convert_fusion.1 = bf16[4096,1536]{1,0:T(8,128)(2,1)} fusion(bf16[4096,640]{1,0:T(8,128)(2,1)} %get-tuple-element.89, bf16[4096,640]{1,0:T(8,128)(2,1)S(1)} %get-tuple-element.88, bf16[768,1920]{1,0:T(8,128)(2,1)} %copy-done.41, bf16[768,1920]{1,0:T(8,128)(2,1)} %copy-done.40), kind=kOutput, calls=%fused_computation.12 | convolution fusion | flops 16141254656 | bytes 28966912 | tf_op jit(solution)/shard_map/dot_general | solution.py:58
  345.1 15.1 %convolution_convert_fusion.5 = bf16[1536,640]{1,0:T(8,128)(2,1)S(1)} fusion(bf16[4096,1536]{1,0:T(8,128)(2,1)} %all-gather.5.cloned.1.call-done, bf16[4096,640]{1,0:T(8,128)(2,1)} %get-tuple-element.31), kind=kOutput, calls=%fused_computation.41 | convolution fusion | flops 8054046720 | bytes 19791872 | tf_op jit(solution)/shard_map/dot_general | solution.py:54
  362.8 17.0 %convolution_convert_fusion.3 = bf16[1536,640]{1,0:T(8,128)(2,1)S(1)} fusion(bf16[4096,1536]{1,0:T(8,128)(2,1)} %all-gather.7.cloned.1.call-done, bf16[4096,640]{1,0:T(8,128)(2,1)} %get-tuple-element.89), kind=kOutput, calls=%fused_computation.39 | convolution fusion | flops 8054046720 | bytes 19791872 | tf_op jit(solution)/shard_map/dot_general | solution.py:54
  382.2 10.7 %convolution_convert_fusion.4 = bf16[1536,640]{1,0:T(8,128)(2,1)S(1)} fusion(bf16[4096,1536]{1,0:T(8,128)(2,1)S(1)} %bitcast.625, bf16[4096,640]{1,0:T(8,128)(2,1)S(1)} %bitcast.585), kind=kOutput, calls=%fused_computation.40 | convolution fusion | flops 8054046720 | bytes 19791872 | tf_op jit(solution)/shard_map/dot_general | solution.py:54
  397.8 9.6 collective-permute-done.17
  409.8 17.9 %collective-permute-done.16 = bf16[768,640]{1,0:T(8,128)(2,1)} collective-permute-done((bf16[768,640]{1,0:T(8,128)(2,1)}, bf16[768,640]{1,0:T(8,128)(2,1)}, u32[]{:S(2)}, u32[]{:S(2)}) %collective-permute-start.16) | collective-permute-done | bytes 983072 | tf_op jit(solution)/shard_map/ppermute | solution.py:63
  429.2 48.9 %reduce-scatter.3.cloned.1.call-done = bf16[256,1536]{1,0:T(8,128)(2,1)} async-done(((bf16[4096,1536]{1,0:T(8,128)(2,1)}), bf16[256,1536]{1,0:T(8,128)(2,1)}) %reduce-scatter.3.cloned.1.call-update) | async-done | bytes 786448 | tf_op jit(solution)/shard_map/reduce_scatter | solution.py:262
  488.5 31.6 %collective-permute-done.18 = bf16[2,2,64,1536]{3,2,1,0:T(8,128)(2,1)S(1)} collective-permute-done((bf16[2,2,64,1536]{3,2,1,0:T(8,128)(2,1)S(1)}, bf16[2,2,64,1536]{3,2,1,0:T(8,128)(2,1)S(1)}, u32[]{:S(2)}, u32[]{:S(2)}) %collective-permute-start.18) | collective-permute-done | bytes 786464 | tf_op jit(solution)/shard_map/ppermute | solution.py:63
  533.9 16.3 %fusion.1 = bf16[2,2,256,3,8,256]{2,5,3,0,4,1:T(8,128)(2,1)} fusion(f32[2,8,256,2,256,3]{4,2,5,3,1,0:T(8,128)} %copy-done.2, f32[2,2,256,3]{2,3,0,1:T(4,128)S(1)} %fusion.45, f32[2,2,256,3]{2,3,0,1:T(4,128)S(1)} %log_add_fusion, pred[2,256,8,256]{1,3,0,2:T(8,128)(4,1)S(1)} %copy-done.28, bf16[8,2,256,128,1,1]{3,2,1,0,5,4:T(8,128)(2,1)} %bitcast.606, ...), kind=kOutput, calls=%fused_computation.4 | convolution fusion | flops 1648361472 | bytes 40656896 | tf_op jit(solution)/shard_map/asrhd,kscd->asrhkc/dot_general | solution.py:301
  559.3 12.1 %fusion.9 = f32[2,128,8,256,1,1]{3,1,5,4,2,0:T(8,128)S(1)} fusion(f32[2,8,256,2,256,3]{4,2,5,3,1,0:T(8,128)} %copy-done.2, f32[2,2,256,3]{2,3,0,1:T(4,128)S(1)} %log_add_fusion, pred[2,256,8,256]{1,3,0,2:T(8,128)(4,1)S(1)} %copy-done.28, bf16[2,2,256,3,128,1]{2,1,0,4,3,5:T(2,128)(2,1)S(1)} %bitcast.592), kind=kOutput, calls=%fused_computation.19 | convolution fusion | flops 1635778560 | bytes 29110272 | tf_op jit(solution)/shard_map/asrhkc,asrhd->kscd/dot_general | solution.py:316
  661.8 34.4 %collective-permute-done.29 = bf16[2,2,64,1536]{3,2,1,0:T(8,128)(2,1)S(1)} collective-permute-done((bf16[2,2,64,1536]{3,2,1,0:T(8,128)(2,1)S(1)}, bf16[2,2,64,1536]{3,2,1,0:T(8,128)(2,1)S(1)}, u32[]{:S(2)}, u32[]{:S(2)}) %collective-permute-start.29) | collective-permute-done | bytes 786464 | tf_op jit(solution)/shard_map/ppermute | solution.py:63
  715.7 15.2 %convolution_convert_fusion = bf16[4096,1536]{1,0:T(8,128)(2,1)} fusion(bf16[4096,640]{1,0:T(8,128)(2,1)} %get-tuple-element.31, bf16[768,1920]{1,0:T(8,128)(2,1)} %copy-done.41, bf16[768,1920]{1,0:T(8,128)(2,1)} %copy-done.40), kind=kOutput, calls=%fused_computation.11 | convolution fusion | flops 8063287296 | bytes 23724032 | tf_op jit(solution)/shard_map/dot_general | solution.py:58
  730.9 20.6 %collective-permute-done.37 = f32[40,128]{1,0:T(8,128)S(1)} collective-permute-done((f32[40,128]{1,0:T(8,128)S(1)}, f32[40,128]{1,0:T(8,128)S(1)}, u32[]{:S(2)}, u32[]{:S(2)}) %collective-permute-start.37) | collective-permute-done | bytes 20512 | tf_op jit(solution)/shard_map/ppermute | solution.py:63
  775.0 23.8 %pad_convert_fusion = f32[768,17920]{1,0:T(8,128)} fusion(bf16[768,512]{1,0:T(8,128)(2,1)S(1)} %get-tuple-element.87), kind=kLoop, calls=%fused_computation.1 | loop fusion | flops 13762560 | bytes 55836672 | tf_op jit(solution)/shard_map/dynamic_update_slice | solution.py:419
  849.2 11.5 %pad_convert_fusion.1 = f32[768,8960]{1,0:T(8,128)} fusion(bf16[768,512]{1,0:T(8,128)(2,1)S(1)} %get-tuple-element.86), kind=kLoop, calls=%fused_computation.13 | loop fusion | flops 6881280 | bytes 28311552 | tf_op jit(solution)/shard_map/dynamic_update_slice | solution.py:419
  901.4 16.8 %collective-permute-done.33 = bf16[768,896]{1,0:T(8,128)(2,1)S(1)} collective-permute-done((bf16[768,896]{1,0:T(8,128)(2,1)S(1)}, bf16[768,896]{1,0:T(8,128)(2,1)S(1)}, u32[]{:S(2)}, u32[]{:S(2)}) %collective-permute-start.33) | collective-permute-done | bytes 1376288 | tf_op jit(solution)/shard_map/ppermute | solution.py:63
  (517 shorter events, 429.3 us)
Async XLA Ops:
  7.2 155.9 %all-gather.5.cloned.1.call-start = ((), (), s32[]{:S(2)}) async-start(), calls=%async_computation.2 | async-start | bytes 13369344 | tf_op jit(solution)/shard_map/all_gather | solution.py:163
  7.9 275.0 %all-gather.7.cloned.1.call-start = ((), (), s32[]{:S(2)}) async-start(), calls=%async_computation.3 | async-start | bytes 13369344 | tf_op jit(solution)/shard_map/all_gather | solution.py:249
  12.3 33.3 %collective-permute-start.2 = (bf16[1,2560]{1,0:T(2,128)(2,1)}, bf16[1,2560]{1,0:T(2,128)(2,1)}, u32[]{:S(2)}, u32[]{:S(2)}) collective-permute-start(bf16[1,2560]{1,0:T(2,128)(2,1)} %broadcast_in_dim.18), channel_id=1, source_target_pairs={{0,16},{16,0},{1,17},{17,1},{2,18},{18,2},{3,19},{19,3},{4,20},{20... | collective-permute-start | bytes 15368 | tf_op jit(solution)/shard_map/ppermute | solution.py:63
  19.6 80.6 %collective-permute-start.12 = (bf16[384,1536]{1,0:T(8,128)(2,1)}, bf16[384,1536]{1,0:T(8,128)(2,1)}, u32[]{:S(2)}, u32[]{:S(2)}) collective-permute-start(bf16[384,1536]{1,0:T(8,128)(2,1)} %constant_dynamic-slice_fusion), channel_id=1, source_target_pairs={{0,16},{16,0},{1,17},{17,1},{2,18},{18,2},{3,19},{19,3},{4,20},{20... | collective-permute-start | bytes 3538952 | tf_op jit(solution)/shard_map/ppermute | solution.py:63
  63.3 33.9 %collective-permute-start.7 = (bf16[1024,128]{0,1:T(8,128)(2,1)S(1)}, bf16[1024,128]{0,1:T(8,128)(2,1)S(1)}, u32[]{:S(2)}, u32[]{:S(2)}) collective-permute-start(bf16[1024,128]{0,1:T(8,128)(2,1)S(1)} %get-tuple-element.42), channel_id=1, source_target_pairs={{8,0},{12,4},{0,8},{4,12},{9,1},{13,5},{1,9},{5,13},{10,2},{14,6},... | collective-permute-start | bytes 786440 | tf_op jit(solution)/shard_map/ppermute | solution.py:68
  100.3 46.9 %collective-permute-start.13 = (bf16[384,1536]{1,0:T(8,128)(2,1)}, bf16[384,1536]{1,0:T(8,128)(2,1)}, u32[]{:S(2)}, u32[]{:S(2)}) collective-permute-start(bf16[384,1536]{1,0:T(8,128)(2,1)} %collective-permute-done.12), channel_id=1, source_target_pairs={{0,1},{1,0},{2,3},{3,2},{4,5},{5,4},{6,7},{7,6},{8,9},{9,8},{10,11... | collective-permute-start | bytes 3538952 | tf_op jit(solution)/shard_map/ppermute | solution.py:63
  163.2 314.9 %reduce-scatter.3.cloned.1.call-start = ((), (), s32[]{:S(2)}) async-start(), calls=%async_computation.4 | async-start | bytes 13369344 | tf_op jit(solution)/shard_map/reduce_scatter | solution.py:262
  169.8 66.3 %collective-permute-start.14 = (bf16[768,1920]{1,0:T(8,128)(2,1)S(1)}, bf16[768,1920]{1,0:T(8,128)(2,1)S(1)}, u32[]{:S(2)}, u32[]{:S(2)}) collective-permute-start(bf16[768,1920]{1,0:T(8,128)(2,1)S(1)} %select_dynamic-update-slice_fusion), channel_id=1, source_target_pairs={{0,16},{16,0},{1,17},{17,1},{2,18},{18,2},{3,19},{19,3},{4,20},{20... | collective-permute-start | bytes 8847368 | tf_op jit(solution)/shard_map/ppermute | solution.py:63
  345.0 422.6 %all-gather.9.cloned.1.call-start = ((), (), s32[]{:S(2)}) async-start(), calls=%async_computation.6 | async-start | bytes 50135040 | tf_op jit(solution)/shard_map/all_gather | solution.py:277
  361.5 34.6 %collective-permute-start.15 = (bf16[768,640]{1,0:T(8,128)(2,1)S(1)}, bf16[768,640]{1,0:T(8,128)(2,1)S(1)}, u32[]{:S(2)}, u32[]{:S(2)}) collective-permute-start(bf16[768,640]{1,0:T(8,128)(2,1)S(1)} %dynamic-slice_bitcast_fusion.3), channel_id=1, source_target_pairs={{0,16},{16,0},{1,17},{17,1},{2,18},{18,2},{3,19},{19,3},{4,20},{20... | collective-permute-start | bytes 2949128 | tf_op jit(solution)/shard_map/ppermute | solution.py:63
  395.2 32.6 %collective-permute-start.16 = (bf16[768,640]{1,0:T(8,128)(2,1)}, bf16[768,640]{1,0:T(8,128)(2,1)}, u32[]{:S(2)}, u32[]{:S(2)}) collective-permute-start(bf16[768,640]{1,0:T(8,128)(2,1)} %dynamic-slice_bitcast_fusion.2), channel_id=1, source_target_pairs={{0,16},{16,0},{1,17},{17,1},{2,18},{18,2},{3,19},{19,3},{4,20},{20... | collective-permute-start | bytes 2949128 | tf_op jit(solution)/shard_map/ppermute | solution.py:63
  485.2 467.9 %reduce-scatter.5.cloned.1.call-start = ((), (), s32[]{:S(2)}) async-start(), calls=%async_computation.5 | async-start | bytes 13369344 | tf_op jit(solution)/shard_map/reduce_scatter | solution.py:373
  487.0 33.1 %collective-permute-start.18 = (bf16[2,2,64,1536]{3,2,1,0:T(8,128)(2,1)S(1)}, bf16[2,2,64,1536]{3,2,1,0:T(8,128)(2,1)S(1)}, u32[]{:S(2)}, u32[]{:S(2)}) collective-permute-start(bf16[2,2,64,1536]{3,2,1,0:T(8,128)(2,1)S(1)} %bitcast.581), channel_id=1, source_target_pairs={{0,2},{2,0},{1,3},{3,1},{4,6},{6,4},{5,7},{7,5},{8,10},{10,8},{9,1... | collective-permute-start | bytes 2359304 | tf_op jit(solution)/shard_map/ppermute | solution.py:63
  581.2 33.9 %collective-permute-start.21 = (bf16[1024,128]{0,1:T(8,128)(2,1)}, bf16[1024,128]{0,1:T(8,128)(2,1)}, u32[]{:S(2)}, u32[]{:S(2)}) collective-permute-start(bf16[1024,128]{0,1:T(8,128)(2,1)} %convert_element_type.742), channel_id=1, source_target_pairs={{4,0},{8,4},{12,8},{0,12},{5,1},{9,5},{13,9},{1,13},{6,2},{10,6},{... | collective-permute-start | bytes 786440 | tf_op jit(solution)/shard_map/ppermute | solution.py:68
  653.2 46.2 %collective-permute-start.24 = (bf16[768,896]{0,1:T(8,128)(2,1)}, bf16[768,896]{0,1:T(8,128)(2,1)}, u32[]{:S(2)}, u32[]{:S(2)}) collective-permute-start(bf16[768,896]{0,1:T(8,128)(2,1)} %dynamic-slice_bitcast_fusion), channel_id=1, source_target_pairs={{0,16},{16,0},{1,17},{17,1},{2,18},{18,2},{3,19},{19,3},{4,20},{20... | collective-permute-start | bytes 4128776 | tf_op jit(solution)/shard_map/ppermute | solution.py:63
  658.4 37.7 %collective-permute-start.29 = (bf16[2,2,64,1536]{3,2,1,0:T(8,128)(2,1)S(1)}, bf16[2,2,64,1536]{3,2,1,0:T(8,128)(2,1)S(1)}, u32[]{:S(2)}, u32[]{:S(2)}) collective-permute-start(bf16[2,2,64,1536]{3,2,1,0:T(8,128)(2,1)S(1)} %fusion.59), channel_id=1, source_target_pairs={{0,2},{2,0},{1,3},{3,1},{4,6},{6,4},{5,7},{7,5},{8,10},{10,8},{9,1... | collective-permute-start | bytes 2359304 | tf_op jit(solution)/shard_map/ppermute | solution.py:63
  710.1 46.0 %collective-permute-start.25 = (bf16[192,896]{1,0:T(8,128)(2,1)S(1)}, bf16[192,896]{1,0:T(8,128)(2,1)S(1)}, u32[]{:S(2)}, u32[]{:S(2)}) collective-permute-start(bf16[192,896]{1,0:T(8,128)(2,1)S(1)} %get-tuple-element.111), channel_id=1, source_target_pairs={{0,4},{4,0},{8,12},{12,8},{1,5},{5,1},{9,13},{13,9},{2,6},{6,2},{1... | collective-permute-start | bytes 1032200 | tf_op jit(solution)/shard_map/ppermute | solution.py:63
  710.2 45.9 %collective-permute-start.27 = (bf16[192,896]{1,0:T(8,128)(2,1)S(1)}, bf16[192,896]{1,0:T(8,128)(2,1)S(1)}, u32[]{:S(2)}, u32[]{:S(2)}) collective-permute-start(bf16[192,896]{1,0:T(8,128)(2,1)S(1)} %get-tuple-element.112), channel_id=1, source_target_pairs={{0,12},{4,8},{8,4},{12,0},{1,13},{5,9},{9,5},{13,1},{2,14},{6,10},... | collective-permute-start | bytes 1032200 | tf_op jit(solution)/shard_map/ppermute | solution.py:63
  714.6 46.6 %collective-permute-start.26 = (bf16[192,896]{1,0:T(8,128)(2,1)S(1)}, bf16[192,896]{1,0:T(8,128)(2,1)S(1)}, u32[]{:S(2)}, u32[]{:S(2)}) collective-permute-start(bf16[192,896]{1,0:T(8,128)(2,1)S(1)} %get-tuple-element.113), channel_id=1, source_target_pairs={{0,8},{4,12},{8,0},{12,4},{1,9},{5,13},{9,1},{13,5},{2,10},{6,14},... | collective-permute-start | bytes 1032200 | tf_op jit(solution)/shard_map/ppermute | solution.py:63
  715.1 36.4 %collective-permute-start.37 = (f32[40,128]{1,0:T(8,128)S(1)}, f32[40,128]{1,0:T(8,128)S(1)}, u32[]{:S(2)}, u32[]{:S(2)}) collective-permute-start(f32[40,128]{1,0:T(8,128)S(1)} %fusion.150), channel_id=1, source_target_pairs={{0,4},{4,0},{8,12},{12,8},{1,5},{5,1},{9,13},{13,9},{2,6},{6,2},{1... | collective-permute-start | bytes 61448 | tf_op jit(solution)/shard_map/ppermute | solution.py:63
  767.6 114.1 %collective-permute-start.32 = (bf16[192,896]{1,0:T(8,128)(2,1)S(1)}, bf16[192,896]{1,0:T(8,128)(2,1)S(1)}, u32[]{:S(2)}, u32[]{:S(2)}) collective-permute-start(bf16[192,896]{1,0:T(8,128)(2,1)S(1)} %fusion.75), channel_id=1, source_target_pairs={{0,4},{4,0},{8,12},{12,8},{1,5},{5,1},{9,13},{13,9},{2,6},{6,2},{1... | collective-permute-start | bytes 1032200 | tf_op jit(solution)/shard_map/ppermute | solution.py:63
  771.2 110.5 %collective-permute-start.31 = (bf16[192,896]{1,0:T(8,128)(2,1)S(1)}, bf16[192,896]{1,0:T(8,128)(2,1)S(1)}, u32[]{:S(2)}, u32[]{:S(2)}) collective-permute-start(bf16[192,896]{1,0:T(8,128)(2,1)S(1)} %fusion.75), channel_id=1, source_target_pairs={{0,8},{4,12},{8,0},{12,4},{1,9},{5,13},{9,1},{13,5},{2,10},{6,14},... | collective-permute-start | bytes 1032200 | tf_op jit(solution)/shard_map/ppermute | solution.py:63
  771.2 110.5 %collective-permute-start.30 = (bf16[192,896]{1,0:T(8,128)(2,1)S(1)}, bf16[192,896]{1,0:T(8,128)(2,1)}, u32[]{:S(2)}, u32[]{:S(2)}) collective-permute-start(bf16[192,896]{1,0:T(8,128)(2,1)S(1)} %fusion.75), channel_id=1, source_target_pairs={{0,12},{4,8},{8,4},{12,0},{1,13},{5,9},{9,5},{13,1},{2,14},{6,10},... | collective-permute-start | bytes 1032200 | tf_op jit(solution)/shard_map/ppermute | solution.py:63
  883.0 35.1 %collective-permute-start.33 = (bf16[768,896]{1,0:T(8,128)(2,1)S(1)}, bf16[768,896]{1,0:T(8,128)(2,1)S(1)}, u32[]{:S(2)}, u32[]{:S(2)}) collective-permute-start(bf16[768,896]{1,0:T(8,128)(2,1)S(1)} %pad_maximum_fusion.18), channel_id=1, source_target_pairs={{0,2},{2,0},{1,3},{3,1},{4,6},{6,4},{5,7},{7,5},{8,10},{10,8},{9,1... | collective-permute-start | bytes 4128776 | tf_op jit(solution)/shard_map/ppermute | solution.py:63
  (120 other events, 2413.0 us)
Sparse Core Ops, SparseCore 0:
  10.3 125.9 all-gather.4
  163.3 119.6 all-gather.6
  345.1 132.9 reduce-scatter.2
  485.3 268.2 all-gather.8
  773.7 134.7 reduce-scatter.4

commit v4 on v3

--- a/solution.py
+++ b/solution.py
@@ -273,15 +273,20 @@
         return total.astype(bf16)
 
     sums_ff = [over_wide(part) for part in (down_part, gate_part, up_part)]
-    grad_normed_mlp, *sums_ff = lax.optimization_barrier((grad_normed_mlp, *sums_ff))
-    ff_all = lax.all_gather(
-        jnp.concatenate(
-            [total[:, :main] for total in sums_ff] + [total[:, main:] for total in sums_ff],
-            axis=1,
-        ),
-        PLANE,
-        axis=0,
-    )
+    left = jnp.concatenate([total[:, main:] for total in sums_ff], axis=1)
+    left = left.reshape(core_count, rows_wide // core_count, -1)
+    theirs = lax.dynamic_index_in_dim(left, 1 - core_at, 0, keepdims=False)
+    left = lax.dynamic_index_in_dim(left, core_at, 0, keepdims=False) + partner(theirs, "core")
+    folds = main // LANES
+    left = left.reshape(folds, -1, 3 * LANES)
+    ff_rows = jnp.concatenate(
+        [
+            jnp.concatenate([total[:, :main] for total in sums_ff], axis=1),
+            jnp.concatenate(list(left), axis=1),
+        ]
+    )
+    grad_normed_mlp, ff_rows = lax.optimization_barrier((grad_normed_mlp, ff_rows))
+    ff_all = lax.all_gather(ff_rows, PLANE, axis=0)
 
     _, scaled_mlp, inverse_mlp = rms_parts(middle, gain_mlp_row)
     grad_middle, grad_gain_mlp = rms_back(
@@ -408,13 +413,18 @@
         [proj_all[c][x, :, q_here : 2 * q_here] for x, c in heads], axis=1
     ).astype(f32)
 
+    tiles = ff_all[: extra * core_count, rows_wide:]
+    tiles = tiles.reshape(extra, core_count, -1, folds, 3 * LANES).transpose(1, 3, 2, 0, 4)
+    tiles = tiles.reshape(rows_wide, extra, 3 * LANES)
+
     def assembled(kinds):
         into = jnp.zeros((rows_wide, len(kinds) * ff), f32)
         at = 0
         for kind in kinds:
-            pieces = [ff_all[p, :, kind * main : (kind + 1) * main] for p in range(share)]
-            first = 3 * main + kind * LANES
-            pieces += [ff_all[e * core_count, :, first : first + LANES] for e in range(extra)]
+            pieces = [
+                ff_all[p, :rows_wide, kind * main : (kind + 1) * main] for p in range(share)
+            ]
+            pieces.append(tiles[:, :, kind * LANES : (kind + 1) * LANES].reshape(rows_wide, -1))
             for piece in pieces:
                 into = lax.dynamic_update_slice(into, piece.astype(f32), (0, at))
                 at += piece.shape[1]

time: 973 us -> 973 us (level)
  local copies, waits for them, and re-layouts: 91.8 us -> 130 us
  waiting for transfers between devices: 350 us -> 324 us
    dynamic_update_slice x45 -> x33, other arithmetic: 150 us -> 123 us  [assembled(): into = lax.dynamic_update_slice(into, piece.astype(f32), (0, at))]
    convert_element_type x1 -> x7, local copies, waits for them, and re-layouts: 1.48 us -> 20.4 us  [assembled(): into = lax.dynamic_update_slice(into, piece.astype(f32), (0, at))]
    reduce_scatter x1, waiting for transfers between devices: 48.9 us -> 32.2 us  [on_device(): lax.psum_scatter(grad_part, PLANE, scatter_dimension=0, tiled=True)]
    concatenate x0 -> x2, other arithmetic: none -> 11.1 us  [the longest x1 11 us: on_device(): jnp.concatenate([jnp.concatenate([total[:, :main] for total in sums_ff],...]
    ppermute x34 -> x35, waiting for transfers between devices: 233 us -> 223 us  [partner(): return lax.ppermute(values, axis, [(i, i ^ distance) for i in range(count)])]
    ppermute x34 -> x35, starting transfers between devices: 39.3 us -> 36 us  [partner(): return lax.ppermute(values, axis, [(i, i ^ distance) for i in range(count)])]
    unnamed x214 -> x223, local copies, waits for them, and re-layouts: 31 us -> 30.4 us
  transfers between devices with their start and end apart: 45 -> 46, of which waited for: 21 -> 22; matrix products, arithmetic and copies ran while one was open for 48% -> 51% of each run, Pallas kernels for 0% -> 0%
where the time goes in v4:
time: 973 us; the launch traced here: 963 us
  waiting for transfers between devices  324 us (33%)
  other arithmetic  252 us (26%)
  matrix products  196 us (20%)
  local copies, waits for them, and re-layouts  130 us (13%)
  starting transfers between devices  45.5 us (5%)
  between operations  15.9 us (2%)
    ppermute x35, waiting for transfers between devices, partner(): return lax.ppermute(values, axis, [(i, i ^ distance) for i in range(count)])  223 us
    dynamic_update_slice x33, other arithmetic, assembled(): into = lax.dynamic_update_slice(into, piece.astype(f32), (0, at))  123 us
    dot_general x5, matrix products, dot_rows(): lax.dot_general(a, b, (((0,), (0,)), ((), ())), preferred_element_type=f32)  49.2 us
    dot_general x4, matrix products, dot(): return jnp.dot(a, b, preferred_element_type=f32)  43.1 us
    dot_general x4, matrix products, dot_cols(): lax.dot_general(a, b, (((1,), (1,)), ((), ())), preferred_element_type=f32)  40.7 us
    ppermute x6, waiting for transfers between devices, shifted(): lax.ppermute(values, axis, [((i + distance) % count, i) for i in range(co...  39.2 us
    ppermute x35, starting transfers between devices, partner(): return lax.ppermute(values, axis, [(i, i ^ distance) for i in range(count)])  36 us
    reduce_scatter x1, waiting for transfers between devices, on_device(): lax.psum_scatter(grad_part, PLANE, scatter_dimension=0, tiled=True)  32.2 us
  transfers between devices with their start and end apart: 46, of which 22 were waited for; matrix products, arithmetic and copies ran while one was open for 51% of the time, Pallas kernels for 0%

profile of v4, /device:TPU:0, one launch (start us, length us, event | category | flops | bytes accessed | tf_op | source)
XLA Modules:
  0.0 963.5 jit_solution(4108577067964588145)
XLA Ops:
  25.9 15.4 %collective-permute-done = bf16[2,2,64,1536]{3,2,1,0:T(8,128)(2,1)} collective-permute-done((bf16[2,2,64,1536]{3,2,1,0:T(8,128)(2,1)}, bf16[2,2,64,1536]{3,2,1,0:T(8,128)(2,1)}, u32[]{:S(2)}, u32[]{:S(2)}) %collective-permute-start) | collective-permute-done | bytes 786464 | tf_op jit(solution)/shard_map/ppermute | solution.py:63
  78.3 19.0 %collective-permute-done.7 = bf16[1024,128]{0,1:T(8,128)(2,1)S(1)} collective-permute-done((bf16[1024,128]{0,1:T(8,128)(2,1)S(1)}, bf16[1024,128]{0,1:T(8,128)(2,1)S(1)}, u32[]{:S(2)}, u32[]{:S(2)}) %collective-permute-start.7) | collective-permute-done | bytes 262176 | tf_op jit(solution)/shard_map/ppermute | solution.py:68
  131.0 13.7 %bitcast_convert_fusion = (bf16[2,2,256,3,128]{2,4,3,0,1:T(8,128)(2,1)S(1)}, f32[2,128,2,256,3,1]{3,1,5,4,2,0:T(8,128)}) fusion(bf16[8,2,256,128,1,1]{3,2,1,0,5,4:T(8,128)(2,1)} %bitcast.557, f32[2,8,256,2,256,3]{4,2,5,3,1,0:T(8,128)} %copy-done.2, f32[2,2,256,3]{2,3,0,1:T(4,128)S(1)} %fusion.2, f32[2,2,256,3]{2,3,0,1:T(4,128)S(1)} %get-tuple-element.157, ...), kind=kOutput, calls=%fused_computation.161 | convolution fusion | flops 1642463232 | bytes 29646848 | tf_op jit(solution)/shard_map/asrhkc,kscd->asrhd/dot_general | solution.py:221
  170.3 65.5 %collective-permute-done.14 = bf16[768,1920]{1,0:T(8,128)(2,1)S(1)} collective-permute-done((bf16[768,1920]{1,0:T(8,128)(2,1)S(1)}, bf16[768,1920]{1,0:T(8,128)(2,1)S(1)}, u32[]{:S(2)}, u32[]{:S(2)}) %collective-permute-start.14) | collective-permute-done | bytes 2949152 | tf_op jit(solution)/shard_map/ppermute | solution.py:63
  238.9 15.6 %fusion.123 = f32[4096,640]{1,0:T(8,128)} fusion(bf16[4096,1536]{1,0:T(8,128)(2,1)} %all-gather.5.cloned.1.call-done, bf16[768,1920]{1,0:T(8,128)(2,1)S(1)} %get-tuple-element.76, bf16[768,1920]{1,0:T(8,128)(2,1)S(1)} %get-tuple-element.75), kind=kOutput, calls=%fused_computation.390 | convolution fusion | flops 8056995840 | bytes 28966912 | tf_op jit(solution)/shard_map/dot_general | solution.py:50
  254.5 28.2 %all-gather.7.cloned.1.call-done = bf16[4096,1536]{1,0:T(8,128)(2,1)} async-done(((bf16[256,1536]{1,0:T(8,128)(2,1)}), bf16[4096,1536]{1,0:T(8,128)(2,1)}) %all-gather.7.cloned.1.call-update) | async-done | bytes 12582928 | tf_op jit(solution)/shard_map/all_gather | solution.py:249
  282.7 23.4 %fusion.47 = f32[4096,1280]{1,0:T(8,128)} fusion(bf16[4096,1536]{1,0:T(8,128)(2,1)} %all-gather.7.cloned.1.call-done, bf16[768,1920]{1,0:T(8,128)(2,1)} %copy-done.46, bf16[768,1920]{1,0:T(8,128)(2,1)} %copy-done.45), kind=kOutput, calls=%fused_computation.176 | convolution fusion | flops 16113991680 | bytes 39452672 | tf_op jit(solution)/shard_map/dot_general | solution.py:50
  306.1 14.1 %multiply_convert_fusion.1 = (bf16[4096,640]{1,0:T(8,128)(2,1)S(1)}, bf16[4096,640]{1,0:T(8,128)(2,1)}, bf16[4096,640]{1,0:T(8,128)(2,1)}) fusion(f32[4096,640]{1,0:T(8,128)S(1)} %copy-done.15, f32[4096,1280]{1,0:T(8,128)} %fusion.47), kind=kLoop, calls=%fused_computation.25 | loop fusion | flops 36700160 | bytes 47185920 | tf_op jit(solution)/shard_map/convert_element_type | solution.py:258
  322.5 22.2 %convolution_convert_fusion.1 = bf16[4096,1536]{1,0:T(8,128)(2,1)} fusion(bf16[4096,640]{1,0:T(8,128)(2,1)} %get-tuple-element.73, bf16[4096,640]{1,0:T(8,128)(2,1)S(1)} %get-tuple-element.72, bf16[768,1920]{1,0:T(8,128)(2,1)} %copy-done.46, bf16[768,1920]{1,0:T(8,128)(2,1)} %copy-done.45), kind=kOutput, calls=%fused_computation.12 | convolution fusion | flops 16141254656 | bytes 28966912 | tf_op jit(solution)/shard_map/dot_general | solution.py:58
  344.8 15.1 %convolution_convert_fusion.5 = bf16[1536,640]{1,0:T(8,128)(2,1)S(1)} fusion(bf16[4096,1536]{1,0:T(8,128)(2,1)} %all-gather.5.cloned.1.call-done, bf16[4096,640]{1,0:T(8,128)(2,1)} %get-tuple-element.27), kind=kOutput, calls=%fused_computation.41 | convolution fusion | flops 8054046720 | bytes 19791872 | tf_op jit(solution)/shard_map/dot_general | solution.py:54
  362.6 17.0 %convolution_convert_fusion.3 = bf16[1536,640]{1,0:T(8,128)(2,1)S(1)} fusion(bf16[4096,1536]{1,0:T(8,128)(2,1)} %all-gather.7.cloned.1.call-done, bf16[4096,640]{1,0:T(8,128)(2,1)} %get-tuple-element.73), kind=kOutput, calls=%fused_computation.39 | convolution fusion | flops 8054046720 | bytes 19791872 | tf_op jit(solution)/shard_map/dot_general | solution.py:54
  382.3 10.7 %convolution_convert_fusion.4 = bf16[1536,640]{1,0:T(8,128)(2,1)S(1)} fusion(bf16[4096,1536]{1,0:T(8,128)(2,1)S(1)} %bitcast.577, bf16[4096,640]{1,0:T(8,128)(2,1)S(1)} %bitcast.535), kind=kOutput, calls=%fused_computation.40 | convolution fusion | flops 8054046720 | bytes 19791872 | tf_op jit(solution)/shard_map/dot_general | solution.py:54
  398.0 9.2 collective-permute-done.17
  409.0 18.5 %collective-permute-done.16 = bf16[768,640]{1,0:T(8,128)(2,1)} collective-permute-done((bf16[768,640]{1,0:T(8,128)(2,1)}, bf16[768,640]{1,0:T(8,128)(2,1)}, u32[]{:S(2)}, u32[]{:S(2)}) %collective-permute-start.16) | collective-permute-done | bytes 983072 | tf_op jit(solution)/shard_map/ppermute | solution.py:63
  434.6 11.0 %maximum_maximum_fusion = bf16[864,1536]{1,0:T(8,128)(2,1)} fusion(bf16[96,384]{1,0:T(8,128)(2,1)S(1)} %get-tuple-element.136, bf16[96,384]{1,0:T(8,128)(2,1)S(1)} %get-tuple-element.137, bf16[96,384]{1,0:T(8,128)(2,1)S(1)} %get-tuple-element.138, bf16[96,384]{1,0:T(8,128)(2,1)S(1)} %get-tuple-element.135, bf16[768,512]{1,0:T(8,128)(2,1)S(1)} %slice-done.3, ...), kind=kLoop, calls=%fused_computation.61 | loop fusion | flops 18579456 | bytes 5308416 | tf_op jit(solution)/shard_map/concatenate | solution.py:282
  445.7 32.2 %reduce-scatter.3.cloned.1.call-done = bf16[256,1536]{1,0:T(8,128)(2,1)} async-done(((bf16[4096,1536]{1,0:T(8,128)(2,1)}), bf16[256,1536]{1,0:T(8,128)(2,1)}) %reduce-scatter.3.cloned.1.call-update) | async-done | bytes 786448 | tf_op jit(solution)/shard_map/reduce_scatter | solution.py:262
  482.2 31.3 %collective-permute-done.19 = bf16[2,2,64,1536]{3,2,1,0:T(8,128)(2,1)S(1)} collective-permute-done((bf16[2,2,64,1536]{3,2,1,0:T(8,128)(2,1)S(1)}, bf16[2,2,64,1536]{3,2,1,0:T(8,128)(2,1)S(1)}, u32[]{:S(2)}, u32[]{:S(2)}) %collective-permute-start.19) | collective-permute-done | bytes 786464 | tf_op jit(solution)/shard_map/ppermute | solution.py:63
  528.0 16.4 %fusion.1 = bf16[2,2,256,3,8,256]{2,5,3,0,4,1:T(8,128)(2,1)} fusion(f32[2,8,256,2,256,3]{4,2,5,3,1,0:T(8,128)} %copy-done.2, f32[2,2,256,3]{2,3,0,1:T(4,128)S(1)} %fusion.45, f32[2,2,256,3]{2,3,0,1:T(4,128)S(1)} %log_add_fusion, pred[2,256,8,256]{1,3,0,2:T(8,128)(4,1)S(1)} %copy-done.33, bf16[8,2,256,128,1,1]{3,2,1,0,5,4:T(8,128)(2,1)} %bitcast.558, ...), kind=kOutput, calls=%fused_computation.4 | convolution fusion | flops 1648361472 | bytes 40656896 | tf_op jit(solution)/shard_map/asrhd,kscd->asrhkc/dot_general | solution.py:306
  553.1 12.0 %fusion.9 = f32[2,128,8,256,1,1]{3,1,5,4,2,0:T(8,128)S(1)} fusion(f32[2,8,256,2,256,3]{4,2,5,3,1,0:T(8,128)} %copy-done.2, f32[2,2,256,3]{2,3,0,1:T(4,128)S(1)} %log_add_fusion, pred[2,256,8,256]{1,3,0,2:T(8,128)(4,1)S(1)} %copy-done.33, bf16[2,2,256,3,128,1]{2,1,0,4,3,5:T(2,128)(2,1)S(1)} %bitcast.542), kind=kOutput, calls=%fused_computation.19 | convolution fusion | flops 1635778560 | bytes 29110272 | tf_op jit(solution)/shard_map/asrhkc,asrhd->kscd/dot_general | solution.py:321
  656.0 34.7 %collective-permute-done.30 = bf16[2,2,64,1536]{3,2,1,0:T(8,128)(2,1)S(1)} collective-permute-done((bf16[2,2,64,1536]{3,2,1,0:T(8,128)(2,1)S(1)}, bf16[2,2,64,1536]{3,2,1,0:T(8,128)(2,1)S(1)}, u32[]{:S(2)}, u32[]{:S(2)}) %collective-permute-start.30) | collective-permute-done | bytes 786464 | tf_op jit(solution)/shard_map/ppermute | solution.py:63
  710.0 15.1 %convolution_convert_fusion = bf16[4096,1536]{1,0:T(8,128)(2,1)} fusion(bf16[4096,640]{1,0:T(8,128)(2,1)} %get-tuple-element.27, bf16[768,1920]{1,0:T(8,128)(2,1)} %copy-done.46, bf16[768,1920]{1,0:T(8,128)(2,1)} %copy-done.45), kind=kOutput, calls=%fused_computation.11 | convolution fusion | flops 8063287296 | bytes 23724032 | tf_op jit(solution)/shard_map/dot_general | solution.py:58
  777.3 19.0 %pad_convert_fusion = f32[768,17920]{1,0:T(8,128)} fusion(bf16[768,512]{1,0:T(8,128)(2,1)S(1)} %get-tuple-element.71), kind=kLoop, calls=%fused_computation.1 | loop fusion | flops 13762560 | bytes 55836672 | tf_op jit(solution)/shard_map/dynamic_update_slice | solution.py:429
  838.0 11.5 %pad_convert_fusion.1 = f32[768,8960]{1,0:T(8,128)} fusion(bf16[768,512]{1,0:T(8,128)(2,1)S(1)} %get-tuple-element.70), kind=kLoop, calls=%fused_computation.13 | loop fusion | flops 6881280 | bytes 28311552 | tf_op jit(solution)/shard_map/dynamic_update_slice | solution.py:429
  876.3 19.7 %collective-permute-done.34 = bf16[768,896]{1,0:T(8,128)(2,1)S(1)} collective-permute-done((bf16[768,896]{1,0:T(8,128)(2,1)S(1)}, bf16[768,896]{1,0:T(8,128)(2,1)S(1)}, u32[]{:S(2)}, u32[]{:S(2)}) %collective-permute-start.34) | collective-permute-done | bytes 1376288 | tf_op jit(solution)/shard_map/ppermute | solution.py:63
  (542 shorter events, 457.1 us)
Async XLA Ops:
  7.2 155.6 %all-gather.5.cloned.1.call-start = ((), (), s32[]{:S(2)}) async-start(), calls=%async_computation.2 | async-start | bytes 13369344 | tf_op jit(solution)/shard_map/all_gather | solution.py:163
  7.9 274.8 %all-gather.7.cloned.1.call-start = ((), (), s32[]{:S(2)}) async-start(), calls=%async_computation.3 | async-start | bytes 13369344 | tf_op jit(solution)/shard_map/all_gather | solution.py:249
  12.3 33.2 %collective-permute-start.2 = (bf16[1,2560]{1,0:T(2,128)(2,1)}, bf16[1,2560]{1,0:T(2,128)(2,1)}, u32[]{:S(2)}, u32[]{:S(2)}) collective-permute-start(bf16[1,2560]{1,0:T(2,128)(2,1)} %broadcast_in_dim.18), channel_id=1, source_target_pairs={{0,16},{16,0},{1,17},{17,1},{2,18},{18,2},{3,19},{19,3},{4,20},{20... | collective-permute-start | bytes 15368 | tf_op jit(solution)/shard_map/ppermute | solution.py:63
  19.6 80.6 %collective-permute-start.12 = (bf16[384,1536]{1,0:T(8,128)(2,1)}, bf16[384,1536]{1,0:T(8,128)(2,1)}, u32[]{:S(2)}, u32[]{:S(2)}) collective-permute-start(bf16[384,1536]{1,0:T(8,128)(2,1)} %constant_dynamic-slice_fusion), channel_id=1, source_target_pairs={{0,16},{16,0},{1,17},{17,1},{2,18},{18,2},{3,19},{19,3},{4,20},{20... | collective-permute-start | bytes 3538952 | tf_op jit(solution)/shard_map/ppermute | solution.py:63
  63.2 34.0 %collective-permute-start.7 = (bf16[1024,128]{0,1:T(8,128)(2,1)S(1)}, bf16[1024,128]{0,1:T(8,128)(2,1)S(1)}, u32[]{:S(2)}, u32[]{:S(2)}) collective-permute-start(bf16[1024,128]{0,1:T(8,128)(2,1)S(1)} %get-tuple-element.38), channel_id=1, source_target_pairs={{8,0},{12,4},{0,8},{4,12},{9,1},{13,5},{1,9},{5,13},{10,2},{14,6},... | collective-permute-start | bytes 786440 | tf_op jit(solution)/shard_map/ppermute | solution.py:68
  65.8 32.0 %collective-permute-start.6 = (bf16[1024,128]{0,1:T(8,128)(2,1)S(1)}, bf16[1024,128]{0,1:T(8,128)(2,1)S(1)}, u32[]{:S(2)}, u32[]{:S(2)}) collective-permute-start(bf16[1024,128]{0,1:T(8,128)(2,1)S(1)} %get-tuple-element.38), channel_id=1, source_target_pairs={{4,0},{8,4},{12,8},{0,12},{5,1},{9,5},{13,9},{1,13},{6,2},{10,6},{... | collective-permute-start | bytes 786440 | tf_op jit(solution)/shard_map/ppermute | solution.py:68
  100.3 46.6 %collective-permute-start.13 = (bf16[384,1536]{1,0:T(8,128)(2,1)}, bf16[384,1536]{1,0:T(8,128)(2,1)}, u32[]{:S(2)}, u32[]{:S(2)}) collective-permute-start(bf16[384,1536]{1,0:T(8,128)(2,1)} %collective-permute-done.12), channel_id=1, source_target_pairs={{0,1},{1,0},{2,3},{3,2},{4,5},{5,4},{6,7},{7,6},{8,9},{9,8},{10,11... | collective-permute-start | bytes 3538952 | tf_op jit(solution)/shard_map/ppermute | solution.py:63
  162.8 315.0 %reduce-scatter.3.cloned.1.call-start = ((), (), s32[]{:S(2)}) async-start(), calls=%async_computation.4 | async-start | bytes 13369344 | tf_op jit(solution)/shard_map/reduce_scatter | solution.py:262
  169.5 66.3 %collective-permute-start.14 = (bf16[768,1920]{1,0:T(8,128)(2,1)S(1)}, bf16[768,1920]{1,0:T(8,128)(2,1)S(1)}, u32[]{:S(2)}, u32[]{:S(2)}) collective-permute-start(bf16[768,1920]{1,0:T(8,128)(2,1)S(1)} %select_dynamic-update-slice_fusion), channel_id=1, source_target_pairs={{0,16},{16,0},{1,17},{17,1},{2,18},{18,2},{3,19},{19,3},{4,20},{20... | collective-permute-start | bytes 8847368 | tf_op jit(solution)/shard_map/ppermute | solution.py:63
  344.8 402.0 %all-gather.9.cloned.1.call-start = ((), (), s32[]{:S(2)}) async-start(), calls=%async_computation.6 | async-start | bytes 45121536 | tf_op jit(solution)/shard_map/all_gather | solution.py:289
  361.3 35.0 %collective-permute-start.15 = (bf16[768,640]{1,0:T(8,128)(2,1)S(1)}, bf16[768,640]{1,0:T(8,128)(2,1)S(1)}, u32[]{:S(2)}, u32[]{:S(2)}) collective-permute-start(bf16[768,640]{1,0:T(8,128)(2,1)S(1)} %dynamic-slice_bitcast_fusion.3), channel_id=1, source_target_pairs={{0,16},{16,0},{1,17},{17,1},{2,18},{18,2},{3,19},{19,3},{4,20},{20... | collective-permute-start | bytes 2949128 | tf_op jit(solution)/shard_map/ppermute | solution.py:63
  395.3 32.2 %collective-permute-start.16 = (bf16[768,640]{1,0:T(8,128)(2,1)}, bf16[768,640]{1,0:T(8,128)(2,1)}, u32[]{:S(2)}, u32[]{:S(2)}) collective-permute-start(bf16[768,640]{1,0:T(8,128)(2,1)} %dynamic-slice_bitcast_fusion.2), channel_id=1, source_target_pairs={{0,16},{16,0},{1,17},{17,1},{2,18},{18,2},{3,19},{19,3},{4,20},{20... | collective-permute-start | bytes 2949128 | tf_op jit(solution)/shard_map/ppermute | solution.py:63
  477.9 474.9 %reduce-scatter.5.cloned.1.call-start = ((), (), s32[]{:S(2)}) async-start(), calls=%async_computation.5 | async-start | bytes 13369344 | tf_op jit(solution)/shard_map/reduce_scatter | solution.py:378
  480.7 32.8 %collective-permute-start.19 = (bf16[2,2,64,1536]{3,2,1,0:T(8,128)(2,1)S(1)}, bf16[2,2,64,1536]{3,2,1,0:T(8,128)(2,1)S(1)}, u32[]{:S(2)}, u32[]{:S(2)}) collective-permute-start(bf16[2,2,64,1536]{3,2,1,0:T(8,128)(2,1)S(1)} %bitcast.531), channel_id=1, source_target_pairs={{0,2},{2,0},{1,3},{3,1},{4,6},{6,4},{5,7},{7,5},{8,10},{10,8},{9,1... | collective-permute-start | bytes 2359304 | tf_op jit(solution)/shard_map/ppermute | solution.py:63
  575.2 33.8 %collective-permute-start.22 = (bf16[1024,128]{0,1:T(8,128)(2,1)}, bf16[1024,128]{0,1:T(8,128)(2,1)}, u32[]{:S(2)}, u32[]{:S(2)}) collective-permute-start(bf16[1024,128]{0,1:T(8,128)(2,1)} %convert_element_type.652), channel_id=1, source_target_pairs={{4,0},{8,4},{12,8},{0,12},{5,1},{9,5},{13,9},{1,13},{6,2},{10,6},{... | collective-permute-start | bytes 786440 | tf_op jit(solution)/shard_map/ppermute | solution.py:68
  648.5 45.4 %collective-permute-start.25 = (bf16[768,896]{0,1:T(8,128)(2,1)}, bf16[768,896]{0,1:T(8,128)(2,1)}, u32[]{:S(2)}, u32[]{:S(2)}) collective-permute-start(bf16[768,896]{0,1:T(8,128)(2,1)} %dynamic-slice_bitcast_fusion), channel_id=1, source_target_pairs={{0,16},{16,0},{1,17},{17,1},{2,18},{18,2},{3,19},{19,3},{4,20},{20... | collective-permute-start | bytes 4128776 | tf_op jit(solution)/shard_map/ppermute | solution.py:63
  653.7 36.9 %collective-permute-start.30 = (bf16[2,2,64,1536]{3,2,1,0:T(8,128)(2,1)S(1)}, bf16[2,2,64,1536]{3,2,1,0:T(8,128)(2,1)S(1)}, u32[]{:S(2)}, u32[]{:S(2)}) collective-permute-start(bf16[2,2,64,1536]{3,2,1,0:T(8,128)(2,1)S(1)} %fusion.59), channel_id=1, source_target_pairs={{0,2},{2,0},{1,3},{3,1},{4,6},{6,4},{5,7},{7,5},{8,10},{10,8},{9,1... | collective-permute-start | bytes 2359304 | tf_op jit(solution)/shard_map/ppermute | solution.py:63
  704.6 28.5 %collective-permute-start.26 = (bf16[192,896]{1,0:T(8,128)(2,1)S(1)}, bf16[192,896]{1,0:T(8,128)(2,1)S(1)}, u32[]{:S(2)}, u32[]{:S(2)}) collective-permute-start(bf16[192,896]{1,0:T(8,128)(2,1)S(1)} %get-tuple-element.98), channel_id=1, source_target_pairs={{0,4},{4,0},{8,12},{12,8},{1,5},{5,1},{9,13},{13,9},{2,6},{6,2},{1... | collective-permute-start | bytes 1032200 | tf_op jit(solution)/shard_map/ppermute | solution.py:63
  708.9 31.4 %collective-permute-start.27 = (bf16[192,896]{1,0:T(8,128)(2,1)S(1)}, bf16[192,896]{1,0:T(8,128)(2,1)S(1)}, u32[]{:S(2)}, u32[]{:S(2)}) collective-permute-start(bf16[192,896]{1,0:T(8,128)(2,1)S(1)} %get-tuple-element.100), channel_id=1, source_target_pairs={{0,8},{4,12},{8,0},{12,4},{1,9},{5,13},{9,1},{13,5},{2,10},{6,14},... | collective-permute-start | bytes 1032200 | tf_op jit(solution)/shard_map/ppermute | solution.py:63
  746.7 109.8 %collective-permute-start.33 = (bf16[192,896]{1,0:T(8,128)(2,1)S(1)}, bf16[192,896]{1,0:T(8,128)(2,1)S(1)}, u32[]{:S(2)}, u32[]{:S(2)}) collective-permute-start(bf16[192,896]{1,0:T(8,128)(2,1)S(1)} %fusion.75), channel_id=1, source_target_pairs={{0,4},{4,0},{8,12},{12,8},{1,5},{5,1},{9,13},{13,9},{2,6},{6,2},{1... | collective-permute-start | bytes 1032200 | tf_op jit(solution)/shard_map/ppermute | solution.py:63
  746.7 109.8 %collective-permute-start.32 = (bf16[192,896]{1,0:T(8,128)(2,1)S(1)}, bf16[192,896]{1,0:T(8,128)(2,1)S(1)}, u32[]{:S(2)}, u32[]{:S(2)}) collective-permute-start(bf16[192,896]{1,0:T(8,128)(2,1)S(1)} %fusion.75), channel_id=1, source_target_pairs={{0,8},{4,12},{8,0},{12,4},{1,9},{5,13},{9,1},{13,5},{2,10},{6,14},... | collective-permute-start | bytes 1032200 | tf_op jit(solution)/shard_map/ppermute | solution.py:63
  749.9 106.6 %collective-permute-start.31 = (bf16[192,896]{1,0:T(8,128)(2,1)S(1)}, bf16[192,896]{1,0:T(8,128)(2,1)}, u32[]{:S(2)}, u32[]{:S(2)}) collective-permute-start(bf16[192,896]{1,0:T(8,128)(2,1)S(1)} %fusion.75), channel_id=1, source_target_pairs={{0,12},{4,8},{8,4},{12,0},{1,13},{5,9},{9,5},{13,1},{2,14},{6,10},... | collective-permute-start | bytes 1032200 | tf_op jit(solution)/shard_map/ppermute | solution.py:63
  857.8 38.2 %collective-permute-start.34 = (bf16[768,896]{1,0:T(8,128)(2,1)S(1)}, bf16[768,896]{1,0:T(8,128)(2,1)S(1)}, u32[]{:S(2)}, u32[]{:S(2)}) collective-permute-start(bf16[768,896]{1,0:T(8,128)(2,1)S(1)} %pad_maximum_fusion.18), channel_id=1, source_target_pairs={{0,2},{2,0},{1,3},{3,1},{4,6},{6,4},{5,7},{7,5},{8,10},{10,8},{9,1... | collective-permute-start | bytes 4128776 | tf_op jit(solution)/shard_map/ppermute | solution.py:63
  898.6 44.3 %collective-permute-start.35 = (bf16[2,768,896]{2,1,0:T(8,128)(2,1)}, bf16[2,768,896]{2,1,0:T(8,128)(2,1)}, u32[]{:S(2)}, u32[]{:S(2)}) collective-permute-start(bf16[2,768,896]{2,1,0:T(8,128)(2,1)} %pad_maximum_fusion.6), channel_id=1, source_target_pairs={{0,1},{1,0},{2,3},{3,2},{4,5},{5,4},{6,7},{7,6},{8,9},{9,8},{10,11... | collective-permute-start | bytes 8257544 | tf_op jit(solution)/shard_map/ppermute | solution.py:63
  (131 other events, 2347.8 us)
Sparse Core Ops, SparseCore 0:
  10.3 125.9 all-gather.4
  162.9 119.7 all-gather.6
  344.9 132.9 reduce-scatter.2
  479.3 238.2 all-gather.8
  756.8 137.9 reduce-scatter.4
